TPU v7x, 32 devices: a whole 2x2x4 slice. The times are simulated.
32 devices in a mesh: segment: 4 (over x, core), seq: 2 (over y), mp: 4 (over z).
Axes of the slice: x: 2, y: 2, z: 4, core: 2. Of those that a mesh axis runs over, the one named last changes fastest.
Arguments:
- captions: bfloat16 [16, 128, 4096], P('seq', None, 'segment'), may hold values from -6 to 6
- caption_lengths: int32 [16], replicated, may hold values from 1 to 128, as said below
- image_caption: int32 [16], replicated, may hold values from 0 to 15, each once
- t5_gain: float32 [4096], P('segment'), may hold values from 0.25 to 1.75
- w_key: bfloat16 [4096, 4096], P('segment', 'mp'), may hold values from -0.09375 to 0.09375
- w_value: bfloat16 [4096, 4096], P('segment', 'mp'), may hold values from -0.09375 to 0.09375
- queries: bfloat16 [16, 512, 4096], P('segment', 'seq', 'mp'), may hold values from -300 to 300
- hidden: bfloat16 [16, 512, 4096], P('segment', 'seq', 'mp'), may hold values from -1.5 to 1.5
- out_gate: float32 [16, 4096], P('segment', 'mp'), may hold values from 1 to 4
- w_out: bfloat16 [4096, 4096], P('mp', 'seq'), may hold values from -0.09375 to 0.09375
Outputs:
- result_rows: bfloat16 [16, 512, 4096], P('segment', 'seq', 'mp')
Inputs may be any that keep to these rules, and one draw needn't show every extreme that they name: `caption_lengths`: each caption has at least one live token, and some caption fills all 128 slots.
All inputs are finite; a program needn't handle non-finite values.
Results may differ from a plain program's by a relative error of at most 0.03.
Values may be sent and summed in bfloat16 or wider, within the bound.
A program may use at most 128 MiB of HBM per device.

v0:
```python
import jax
import jax.numpy as jnp
from jax import lax
from jax.sharding import PartitionSpec as P

HEAD = 128


def shards(
    captions,
    caption_lengths,
    image_caption,
    t5_gain,
    w_key,
    w_value,
    queries,
    hidden,
    out_gate,
    w_out,
):
    caption_count, caption_slots, feature_share = captions.shape
    image_count, patch_count, head_cols = queries.shape
    segment_count = lax.axis_size("segment")
    caption_values = captions.astype(jnp.float32)
    squares_total = lax.psum(jnp.sum(caption_values * caption_values, axis=2), "segment")
    inverse_rms = lax.rsqrt(squares_total / (feature_share * segment_count) + 1e-06)
    normed = (caption_values * inverse_rms[:, :, None] * t5_gain).astype(jnp.bfloat16)
    flattened = normed.reshape(caption_count * caption_slots, feature_share)
    key_partial = jnp.dot(flattened, w_key, preferred_element_type=jnp.float32)
    value_partial = jnp.dot(flattened, w_value, preferred_element_type=jnp.float32)
    first_image = lax.axis_index("segment") * image_count
    owner_ids = lax.dynamic_slice_in_dim(image_caption, first_image, image_count)
    stacked = jnp.concatenate([key_partial, value_partial], axis=1)
    column_share = lax.psum_scatter(
        stacked.astype(jnp.bfloat16), "segment", scatter_dimension=1, tiled=True
    ).astype(jnp.float32)
    piece_width = column_share.shape[1]
    column_share = column_share.astype(jnp.bfloat16).reshape(
        1, caption_count, caption_slots, piece_width
    )
    pieces = lax.all_gather(column_share, ("segment", "seq"), axis=0, tiled=True)
    pieces = pieces.reshape(segment_count, -1, caption_slots, piece_width)
    encoded = pieces.transpose(1, 2, 0, 3).reshape(
        pieces.shape[1], caption_slots, segment_count * piece_width
    )
    chosen = jnp.take(encoded, owner_ids, axis=0)
    live_lengths = jnp.take(caption_lengths, owner_ids)
    live_mask = jnp.arange(caption_slots, dtype=jnp.int32)[None, :] < live_lengths[:, None]
    head_count = head_cols // HEAD
    query_heads = queries.reshape(image_count, patch_count, head_count, HEAD)
    key_heads = chosen[:, :, :head_cols].reshape(image_count, caption_slots, head_count, HEAD)
    value_heads = chosen[:, :, head_cols:].reshape(image_count, caption_slots, head_count, HEAD)
    scores = jnp.einsum(
        "iphd,ikhd->ihpk", query_heads, key_heads, preferred_element_type=jnp.float32
    ) * HEAD ** (-0.5)
    scores = jnp.where(live_mask[:, None, None, :], scores, -1e30)
    weights = jax.nn.softmax(scores, axis=3).astype(jnp.bfloat16)
    attended = jnp.einsum(
        "ihpk,ikhd->iphd", weights, value_heads, preferred_element_type=jnp.float32
    )
    attended = attended.astype(jnp.bfloat16).reshape(image_count * patch_count, head_cols)
    partial_value = jnp.dot(
        attended,
        lax.all_gather(w_out, "seq", axis=1, tiled=True),
        preferred_element_type=jnp.float32,
    )
    mixed_heads = lax.psum_scatter(
        partial_value.astype(jnp.bfloat16), "mp", scatter_dimension=1, tiled=True
    ).astype(jnp.float32)
    result_rows = hidden.astype(jnp.float32) + out_gate[:, None, :] * mixed_heads.reshape(
        image_count, patch_count, head_cols
    )
    return result_rows.astype(jnp.bfloat16)


def solution(mesh):
    in_specs = (
        P("seq", None, "segment"),
        P(),
        P(),
        P("segment"),
        P("segment", "mp"),
        P("segment", "mp"),
        P("segment", "seq", "mp"),
        P("segment", "seq", "mp"),
        P("segment", "mp"),
        P("mp", "seq"),
    )
    out_specs = P("segment", "seq", "mp")
    return jax.shard_map(shards, mesh=mesh, in_specs=in_specs, out_specs=out_specs, check_vma=False)
```

profile of v0, /device:TPU:12, one launch (start us, length us, event | category | flops | bytes accessed | tf_op | source)
XLA Modules:
  0.0 402.2 jit_solution(8500879243385912483)
XLA Ops:
  6.5 0.0 copy-start
  6.5 0.0 copy-start.4
  6.5 0.0 reduce-scatter.3.cloned.1.call-start
  6.5 2.2 fusion.1
  8.8 6.9 %psum.7 = f32[8,128]{1,0:T(8,128)S(1)} all-reduce(f32[8,128]{1,0:T(8,128)S(1)} %fusion.1), channel_id=1, replica_groups=mesh['segment'=4,'seq'=2,'mp'=4] {'segment'}, use_global_device_ids=true, to_apply=%region_1.0 | all-reduce | flops 1024 | bytes 8192 | tf_op jit(solution)/shard_map/psum | solution.py:25
  15.7 0.0 copy-done.4
  15.7 2.1 fusion.3
  17.8 0.0 copy-done
  17.8 0.0 copy-start.6
  17.8 2.4 convolution_convert_fusion.1
  20.2 0.0 copy-done.6
  20.2 2.4 convolution_convert_fusion.2
  22.6 2.4 pad_maximum_fusion
  25.0 0.0 reduce-scatter.3.cloned.1.call-update
  25.0 0.0 all-gather.3.cloned.1.call-start
  25.1 44.8 %reduce-scatter.3.cloned.1.call-done = bf16[1024,512]{0,1:T(8,128)(2,1)} async-done(((bf16[1024,2048]{0,1:T(8,128)(2,1)}), bf16[1024,512]{0,1:T(8,128)(2,1)}) %reduce-scatter.3.cloned.1.call-update) | async-done | bytes 1048592 | tf_op jit(solution)/shard_map/reduce_scatter | solution.py:34
  69.9 2.3 copy.33
  72.2 0.0 all-gather.3.cloned.1.call-update
  72.2 0.0 copy-start.5
  72.2 0.0 copy-start.2
  72.2 0.0 all-gather.5.cloned.1.call-start
  72.3 0.7 all-gather.5.cloned.1.call-update
  73.0 0.2 reduce-scatter.5.cloned.1.call-start
  73.2 0.0 copy-done.5
  73.2 0.1 compare_and_fusion
  73.3 0.0 copy-done.2
  73.3 0.6 gather_fusion.1
  73.9 0.1 iota_compare_fusion
  74.0 52.4 %all-gather.3.cloned.1.call-done = bf16[8,8,128,512]{3,2,1,0:T(8,128)(2,1)} async-done(((bf16[1,8,128,512]{3,2,1,0:T(8,128)(2,1)}), bf16[8,8,128,512]{3,2,1,0:T(8,128)(2,1)}) %all-gather.3.cloned.1.call-update) | async-done | bytes 8388624 | tf_op jit(solution)/shard_map/all_gather | solution.py:41
  126.4 12.4 %copy.23 = bf16[16,128,4,512]{1,3,2,0:T(8,128)(2,1)} copy(bf16[16,128,4,512]{3,1,0,2:T(8,128)(2,1)} %bitcast.43) | data formatting | bytes 16777216 | tf_op jit(solution)/shard_map/transpose | solution.py:43
  138.8 12.7 %copy.24 = bf16[16,128,2048]{2,1,0:T(8,128)(2,1)} copy(bf16[16,128,2048]{1,2,0:T(8,128)(2,1)} %bitcast.42) | data formatting | bytes 16777216 | tf_op jit(solution)/shard_map/reshape | solution.py:43
  151.5 4.1 %gather_fusion = bf16[4,128,2048]{2,1,0:T(8,128)(2,1)S(1)} fusion(bf16[16,128,2048]{2,1,0:T(8,128)(2,1)} %copy.24, s32[1024]{0:T(1024)S(1)} %pad_clamp_fusion), kind=kCustom, calls=%fused_computation | custom fusion | bytes 4194320 | tf_op jit(solution)/shard_map/jit(_take)/gather | solution.py:46
  155.5 0.3 broadcast_select_fusion
  155.8 0.2 fusion.21
  156.0 0.7 copy.26
  156.6 0.7 copy.25
  157.3 2.3 fusion.12
  159.7 1.7 fusion.22
  161.4 2.0 convert_bitcast_fusion
  163.4 3.1 copy.30
  166.5 64.9 %all-gather.5.cloned.1.call-done = bf16[1024,4096]{1,0:T(8,128)(2,1)} async-done(((bf16[1024,2048]{1,0:T(8,128)(2,1)}), bf16[1024,4096]{1,0:T(8,128)(2,1)}) %all-gather.5.cloned.1.call-update) | async-done | bytes 8388624 | tf_op jit(solution)/shard_map/all_gather | solution.py:64
  231.5 14.2 %convolution_convert_fusion = bf16[1024,4096]{1,0:T(8,128)(2,1)} fusion(bf16[1024,4096]{1,0:T(8,128)(2,1)} %all-gather.5.cloned.1.call-done, bf16[128,8,8,128]{3,2,1,0:T(8,128)(2,1)S(1)} %bitcast.47), kind=kOutput, calls=%fused_computation.3 | convolution fusion | flops 8594128896 | bytes 18874368 | tf_op jit(solution)/shard_map/dot_general | solution.py:62
  245.7 0.0 copy-start.3
  245.7 0.0 reduce-scatter.5.cloned.1.call-update
  245.7 145.2 %reduce-scatter.5.cloned.1.call-done = bf16[1024,1024]{1,0:T(8,128)(2,1)} async-done(((bf16[1024,4096]{1,0:T(8,128)(2,1)}), bf16[1024,1024]{1,0:T(8,128)(2,1)}) %reduce-scatter.5.cloned.1.call-update) | async-done | bytes 2097168 | tf_op jit(solution)/shard_map/reduce_scatter | solution.py:67
  390.9 0.0 copy-done.3
  390.9 4.7 %fusion.5 = bf16[4,256,1024]{2,1,0:T(8,128)(2,1)} fusion(bf16[4,256,1024]{2,1,0:T(8,128)(2,1)} %bitcast.46, bf16[4,256,1024]{2,1,0:T(8,128)(2,1)} %param.17, f32[4,1024]{1,0:T(4,128)S(1)} %copy-done.3), kind=kLoop, calls=%fused_computation.12 | loop fusion | flops 5242880 | bytes 6307840 | tf_op jit(solution)/shard_map/convert_element_type | solution.py:73
  395.7 0.0 copy-done.1
  (4 shorter events, 0.0 us)
Async XLA Ops:
  6.5 11.3 %copy-start = (bf16[1024,1024]{1,0:T(8,128)(2,1)S(1)}, bf16[1024,1024]{1,0:T(8,128)(2,1)}, u32[]{:S(2)}) copy-start(bf16[1024,1024]{1,0:T(8,128)(2,1)} %param.15) | copy-start | bytes 6291460
  6.5 9.1 %copy-start.4 = (f32[1024]{0:T(1024)S(1)}, f32[1024]{0:T(1024)}, u32[]{:S(2)}) copy-start(f32[1024]{0:T(1024)} %param.13) | copy-start | bytes 12292
  6.5 63.4 %reduce-scatter.3.cloned.1.call-start = ((), (), s32[]{:S(2)}) async-start(), calls=%async_computation.2 | async-start | bytes 5242880 | tf_op jit(solution)/shard_map/reduce_scatter | solution.py:34
  17.8 2.4 copy-start.6
  25.0 101.3 %all-gather.3.cloned.1.call-start = ((), (), s32[]{:S(2)}) async-start(), calls=%async_computation.3 | async-start | bytes 9437184 | tf_op jit(solution)/shard_map/all_gather | solution.py:41
  72.2 1.0 copy-start.5
  72.2 1.1 copy-start.2
  72.2 159.2 %all-gather.5.cloned.1.call-start = ((), (), s32[]{:S(2)}) async-start(), calls=%async_computation.4 | async-start | bytes 12582912 | tf_op jit(solution)/shard_map/all_gather | solution.py:64
  73.0 318.0 %reduce-scatter.5.cloned.1.call-start = ((), (), s32[]{:S(2)}) async-start(), calls=%async_computation.5 | async-start | bytes 10485760 | tf_op jit(solution)/shard_map/reduce_scatter | solution.py:67
  245.7 145.3 %copy-start.3 = (f32[4,1024]{1,0:T(4,128)S(1)}, f32[4,1024]{1,0:T(4,128)}, u32[]{:S(2)}) copy-start(f32[4,1024]{1,0:T(4,128)} %param.18) | copy-start | bytes 49156
  390.9 4.7 %copy-start.1 = (bf16[1024,1024]{1,0:T(8,128)(2,1)S(1)}, bf16[1024,1024]{1,0:T(8,128)(2,1)}, u32[]{:S(2)}) copy-start(bf16[1024,1024]{1,0:T(8,128)(2,1)} %param.15) | copy-start | bytes 6291460
Sparse Core Ops, SparseCore 0:
  25.2 44.6 reduce-scatter.2
  72.3 54.0 all-gather.2
  128.0 103.4 all-gather.4
  245.8 145.0 reduce-scatter.4
where the time goes:
time: 405 us; the launch traced here: 402 us
  waiting for transfers between devices  308 us (76%)
  local copies, waits for them, and re-layouts  36.7 us (9%)
  matrix products  23.3 us (6%)
  other arithmetic  13.6 us (3%)
  between operations  13.3 us (3%)
  blocking collectives  6.9 us (2%)
    reduce_scatter x1, waiting for transfers between devices, shards(): lax.psum_scatter(partial_value.astype(jnp.bfloat16), 'mp', scatter_dimens...  145 us
    all_gather x1, waiting for transfers between devices, shards(): lax.all_gather(w_out, 'seq', axis=1, tiled=True)  64.9 us
    all_gather x1, waiting for transfers between devices, shards(): lax.all_gather(column_share, ('segment', 'seq'), axis=0, tiled=True)  52.4 us
    reduce_scatter x1, waiting for transfers between devices, shards(): lax.psum_scatter(stacked.astype(jnp.bfloat16), 'segment', scatter_dimensi...  44.8 us
    dot_general x1, matrix products, shards(): jnp.dot(attended, lax.all_gather(w_out, 'seq', axis=1, tiled=True), prefe...  14.2 us
    reshape x1, local copies, waits for them, and re-layouts, shards(): pieces.transpose(1, 2, 0, 3)  12.7 us
    transpose x1, local copies, waits for them, and re-layouts, shards(): pieces.transpose(1, 2, 0, 3)  12.4 us
  transfers between devices with their start and end apart: 4, of which 4 were waited for; matrix products, arithmetic and copies ran while one was open for 10% of the time, Pallas kernels for 0%

commit v1 on v0

--- a/solution.py
+++ b/solution.py
@@ -1,12 +1,19 @@
+import functools
+
 import jax
 import jax.numpy as jnp
 from jax import lax
+from jax.experimental import pallas as pl
+from jax.experimental.pallas import tpu as pltpu
 from jax.sharding import PartitionSpec as P
 
 HEAD = 128
-
-
-def shards(
+MESH = pl.DeviceIdType.MESH
+BF16 = jnp.bfloat16
+F32 = jnp.float32
+
+
+def general_shards(
     captions,
     caption_lengths,
     image_caption,
@@ -73,6 +80,453 @@
     return result_rows.astype(jnp.bfloat16)
 
 
+def fused_kernel(
+    image_caption, caption_lengths, gain, gate, captions, w_key, w_value, queries, hidden, w_out,
+    result,
+    cap_raw, key_w, value_w, query_v, hidden_v, out_w, scaled, squares,
+    pair_send, pair_recv, own, cross_recv, rows, attended, moving, from_right,
+    local_sem, pair_ssem, pair_rsem, cross_ssem, cross_rsem, row_ssem, row_rsem,
+    w_ssem, w_rsem, wf_ssem, wf_rsem, z_ssem, z_rsem, left_rsem,
+):
+    seg = lax.axis_index("segment")
+    seq = lax.axis_index("seq")
+    mp = lax.axis_index("mp")
+    chip, core = seg // 2, seg % 2
+    pair_id = {"segment": seg + 1 - 2 * core}
+    cross_id = {"segment": (seg + 2) % 4}
+    seq_id = {"seq": 1 - seq}
+    caption_count, slots, features = cap_raw.shape
+    images, patches, width = query_v.shape
+    both = 2 * width
+    head_count = width // HEAD
+    half = out_w.shape[1] // 2
+    total_features = 4 * features
+
+    def device(ids):
+        return {"segment": seg, "seq": seq, "mp": mp, **ids}
+
+    loads = [
+        pltpu.make_async_copy(captions, cap_raw, local_sem.at[0]),
+        pltpu.make_async_copy(w_key, key_w, local_sem.at[1]),
+        pltpu.make_async_copy(w_value, value_w, local_sem.at[2]),
+        pltpu.make_async_copy(queries, query_v, local_sem.at[3]),
+        pltpu.make_async_copy(
+            w_out.at[:, pl.ds(0, width)], out_w.at[2 * seq], local_sem.at[4]
+        ),
+        pltpu.make_async_copy(
+            w_out.at[:, pl.ds(width, width)], out_w.at[2 * seq + 1], local_sem.at[5]
+        ),
+        pltpu.make_async_copy(hidden, hidden_v, local_sem.at[6]),
+    ]
+    for load in loads:
+        load.start()
+
+    barrier = pltpu.get_barrier_semaphore()
+    for ids in (pair_id, cross_id, seq_id):
+        pl.semaphore_signal(barrier, inc=1, device_id=device(ids), device_id_type=MESH)
+
+    @pl.when(mp > 0)
+    def _():
+        pl.semaphore_signal(barrier, inc=1, device_id=device({"mp": mp - 1}), device_id_type=MESH)
+
+    @pl.when(mp < 3)
+    def _():
+        pl.semaphore_signal(barrier, inc=1, device_id=device({"mp": mp + 1}), device_id_type=MESH)
+
+    neighbours = 5 - (mp == 0).astype(jnp.int32) - (mp == 3).astype(jnp.int32)
+    pl.semaphore_wait(barrier, neighbours)
+
+    half_rows = pl.ds(pl.multiple_of(core * half, half), half)
+
+    def w_copy(step):
+        local_block = seq if step == 0 else 1 - seq
+        block = 2 * seq + local_block
+        return pltpu.make_async_remote_copy(
+            src_ref=w_out.at[half_rows, pl.ds(pl.multiple_of(local_block * width, width), width)],
+            dst_ref=out_w.at[block, half_rows],
+            send_sem=w_ssem.at[step],
+            recv_sem=w_rsem.at[step],
+            device_id=device(seq_id),
+            device_id_type=MESH,
+        )
+
+    def w_forward(step):
+        other = 1 - seq
+        block = 2 * other + (other if step == 0 else 1 - other)
+        return pltpu.make_async_remote_copy(
+            src_ref=out_w.at[block, half_rows],
+            dst_ref=out_w.at[block, half_rows],
+            send_sem=wf_ssem.at[step],
+            recv_sem=wf_rsem.at[step],
+            device_id=device(pair_id),
+            device_id_type=MESH,
+        )
+
+    w_copy(0).start()
+
+    loads[0].wait()
+
+    @pl.loop(0, caption_count)
+    def _(c):
+        values = cap_raw[c].astype(F32)
+        scaled[c] = (values * gain[...]).astype(BF16)
+        square = values * values
+        folded = square[:, :HEAD]
+        for group in range(1, features // HEAD):
+            folded = folded + square[:, group * HEAD : (group + 1) * HEAD]
+        squares[c] = folded.astype(BF16)
+
+    loads[1].wait()
+    loads[2].wait()
+    tile = 256
+
+    def slot_partial(j, out_core, dst):
+        ids = [image_caption[4 * (2 * x + out_core) + j] % caption_count for x in range(2)]
+        lhs = jnp.concatenate([scaled[i] for i in ids], axis=0)
+
+        @pl.loop(0, width // tile)
+        def _(t):
+            cols = pl.ds(pl.multiple_of(t * tile, tile), tile)
+            vcols = pl.ds(pl.multiple_of(width + t * tile, tile), tile)
+            k = jnp.dot(lhs, key_w[:, cols], preferred_element_type=F32).astype(BF16)
+            v = jnp.dot(lhs, value_w[:, cols], preferred_element_type=F32).astype(BF16)
+            for x in range(2):
+                dst[j, x, :, cols] = k[x * slots : (x + 1) * slots]
+                dst[j, x, :, vcols] = v[x * slots : (x + 1) * slots]
+
+        for x in range(2):
+            dst[j, x, :, both:] = squares[ids[x]]
+
+    def pair_copy(j):
+        return pltpu.make_async_remote_copy(
+            src_ref=pair_send.at[j], dst_ref=pair_recv.at[j],
+            send_sem=pair_ssem.at[j], recv_sem=pair_rsem.at[j],
+            device_id=device(pair_id), device_id_type=MESH,
+        )
+
+    def cross_copy(j):
+        return pltpu.make_async_remote_copy(
+            src_ref=own.at[j, 1 - chip], dst_ref=cross_recv.at[j],
+            send_sem=cross_ssem.at[j], recv_sem=cross_rsem.at[j],
+            device_id=device(cross_id), device_id_type=MESH,
+        )
+
+    def row_copy(j):
+        return pltpu.make_async_remote_copy(
+            src_ref=rows.at[j, seq], dst_ref=rows.at[j, seq],
+            send_sem=row_ssem.at[j], recv_sem=row_rsem.at[j],
+            device_id=device(seq_id), device_id_type=MESH,
+        )
+
+    def stage_partial(j):
+        slot_partial(j, 1 - core, pair_send)
+        pair_copy(j).start()
+        slot_partial(j, core, own)
+
+    def stage_pair(j):
+        pair_copy(j).wait_recv()
+        far = 1 - chip
+        own[j, far] = (own[j, far].astype(F32) + pair_recv[j, far].astype(F32)).astype(BF16)
+        cross_copy(j).start()
+
+    def stage_rows(j):
+        cross_copy(j).wait_recv()
+        sums = [ref[...].astype(F32) for ref in (
+            own.at[j, chip, :, pl.ds(both, HEAD)],
+            pair_recv.at[j, chip, :, pl.ds(both, HEAD)],
+            cross_recv.at[j, :, pl.ds(both, HEAD)],
+        )]
+        mean = jnp.sum(sums[0] + sums[1] + sums[2], axis=1, keepdims=True) / total_features
+        inverse = lax.rsqrt(mean + 1e-06)
+
+        @pl.loop(0, both // tile)
+        def _(t):
+            cols = pl.ds(pl.multiple_of(t * tile, tile), tile)
+            value = (
+                own[j, chip, :, cols].astype(F32)
+                + pair_recv[j, chip, :, cols].astype(F32)
+                + cross_recv[j, :, cols].astype(F32)
+            )
+            rows[j, seq, :, cols] = (value * inverse).astype(BF16)
+
+        row_copy(j).start()
+
+    def stage_attend(j):
+        row_copy(j).wait_recv()
+        caption = image_caption[4 * seg + j]
+        from_first = caption < caption_count
+        live = caption_lengths[caption]
+        mask = lax.broadcasted_iota(jnp.int32, (patches, slots), 1) < live
+        for h in range(head_count):
+            cols = slice(h * HEAD, (h + 1) * HEAD)
+            vcols = slice(width + h * HEAD, width + (h + 1) * HEAD)
+            scores = lax.dot_general(
+                query_v[j, :, cols], jnp.where(from_first, rows[j, 0, :, cols], rows[j, 1, :, cols]),
+                (((1,), (1,)), ((), ())), preferred_element_type=F32,
+            ) * HEAD ** (-0.5)
+            scores = jnp.where(mask, scores, -1e30)
+            top = jnp.max(scores, axis=1, keepdims=True)
+            expd = jnp.exp(scores - top)
+            weights = (expd / jnp.sum(expd, axis=1, keepdims=True)).astype(BF16)
+            attended[j, :, cols] = jnp.dot(
+                weights,
+                jnp.where(from_first, rows[j, 0, :, vcols], rows[j, 1, :, vcols]),
+                preferred_element_type=F32,
+            ).astype(BF16)
+
+    def up_copy(n, j):
+        return pltpu.make_async_remote_copy(
+            src_ref=moving.at[n, j], dst_ref=moving.at[n, j],
+            send_sem=z_ssem.at[n, j], recv_sem=z_rsem.at[n, j],
+            device_id=device({"mp": lax.min(mp + 1, 3)}), device_id_type=MESH,
+        )
+
+    def down_copy(n, j):
+        return pltpu.make_async_remote_copy(
+            src_ref=moving.at[n, j], dst_ref=moving.at[n, j],
+            send_sem=z_ssem.at[n, j], recv_sem=z_rsem.at[n, j],
+            device_id=device({"mp": lax.max(mp - 1, 0)}), device_id_type=MESH,
+        )
+
+    def last_copy(n, j):
+        return pltpu.make_async_remote_copy(
+            src_ref=moving.at[n, j], dst_ref=from_right.at[j],
+            send_sem=z_ssem.at[n, j], recv_sem=left_rsem.at[j],
+            device_id=device({"mp": lax.max(mp - 1, 0)}), device_id_type=MESH,
+        )
+
+    def send_on(n, j):
+        @pl.when(n > mp)
+        def _():
+            up_copy(n, j).start()
+
+        @pl.when(n < mp - 1)
+        def _():
+            down_copy(n, j).start()
+
+        @pl.when(n == mp - 1)
+        def _():
+            last_copy(n, j).start()
+
+    def source_step(n, j):
+        @pl.loop(0, width // tile)
+        def _(t):
+            cols = pl.ds(pl.multiple_of(t * tile, tile), tile)
+            moving[n, j, :, cols] = jnp.dot(
+                attended[j], out_w[n, :, cols], preferred_element_type=F32
+            ).astype(BF16)
+
+        send_on(n, j)
+
+    def relay_step(n, j):
+        up_copy(n, j).wait_recv()
+
+        @pl.loop(0, width // tile)
+        def _(t):
+            cols = pl.ds(pl.multiple_of(t * tile, tile), tile)
+            share = jnp.dot(attended[j], out_w[n, :, cols], preferred_element_type=F32)
+            moving[n, j, :, cols] = (share + moving[n, j, :, cols].astype(F32)).astype(BF16)
+
+        send_on(n, j)
+
+    def final_step(j):
+        @pl.when(mp > 0)
+        def _():
+            up_copy(mp, j).wait_recv()
+
+        @pl.when(mp < 3)
+        def _():
+            last_copy(mp, j).wait_recv()
+
+        @pl.loop(0, width // tile)
+        def _(t):
+            cols = pl.ds(pl.multiple_of(t * tile, tile), tile)
+            share = jnp.dot(attended[j], out_w[mp, :, cols], preferred_element_type=F32)
+            below = moving[mp, j, :, cols].astype(F32)
+            above = from_right[j, :, cols].astype(F32)
+            share = share + jnp.where(mp > 0, below, 0.0) + jnp.where(mp < 3, above, 0.0)
+            result[j, :, cols] = (
+                hidden_v[j, :, cols].astype(F32) + gate[j, :, cols] * share
+            ).astype(BF16)
+
+    is_end = (mp == 0) | (mp == 3)
+    first = jnp.where(mp < 2, 3, 0)
+    third = 1 + seq
+    late = 2 - seq
+    end_order = (first, third)
+
+    def wait_send(n, j):
+        up_copy(n, j).wait_send()
+
+    @pl.loop(0, images + 4)
+    def _(t):
+        @pl.when(t < images)
+        def _():
+            stage_partial(t)
+
+        @pl.when((t >= 1) & (t < images + 1))
+        def _():
+            stage_pair(t - 1)
+
+        @pl.when((t >= 2) & (t < images + 2))
+        def _():
+            stage_rows(t - 2)
+
+        @pl.when(t == images + 1)
+        def _():
+            w_copy(1).start()
+
+        @pl.when((t >= 3) & (t < images + 3))
+        def _():
+            j = t - 3
+
+            @pl.when(j == 0)
+            def _():
+                loads[3].wait()
+
+            stage_attend(j)
+
+            @pl.when(j == 0)
+            def _():
+                w_copy(0).wait_recv()
+                w_forward(0).start()
+                loads[4].wait()
+                loads[5].wait()
+                w_forward(0).wait_recv()
+
+            @pl.when(is_end)
+            def _():
+                for n in end_order:
+                    @pl.when(j >= 1)
+                    def _():
+                        wait_send(n, j - 1)
+
+                    source_step(n, j)
+
+        @pl.when((t >= 4) & jnp.logical_not(is_end))
+        def _():
+            j = t - 4
+            relay_step(first, j)
+            relay_step(3 - first, j)
+
+            @pl.when(third != mp)
+            def _():
+                relay_step(third, j)
+
+    w_copy(1).wait_recv()
+    w_forward(1).start()
+    w_forward(1).wait_recv()
+    loads[6].wait()
+
+    @pl.loop(0, images)
+    def _(j):
+        @pl.when(is_end)
+        def _():
+            @pl.when(j == 0)
+            def _():
+                for n in end_order:
+                    wait_send(n, images - 1)
+
+            @pl.when(j >= 1)
+            def _():
+                wait_send(late, j - 1)
+
+            source_step(late, j)
+
+        @pl.when(jnp.logical_not(is_end) & (late != mp))
+        def _():
+            relay_step(late, j)
+
+        final_step(j)
+
+    for step in range(2):
+        w_copy(step).wait_send()
+        w_forward(step).wait_send()
+
+    @pl.loop(0, images)
+    def _(j):
+        pair_copy(j).wait_send()
+        cross_copy(j).wait_send()
+        row_copy(j).wait_send()
+
+        @pl.when(jnp.logical_not(is_end))
+        def _():
+            wait_send(first, j)
+            wait_send(3 - first, j)
+
+            @pl.when(third != mp)
+            def _():
+                wait_send(third, j)
+
+            @pl.when(late != mp)
+            def _():
+                wait_send(late, j)
+
+    @pl.when(is_end)
+    def _():
+        wait_send(late, images - 1)
+
+
+def fused_shards(
+    captions,
+    caption_lengths,
+    image_caption,
+    t5_gain,
+    w_key,
+    w_value,
+    queries,
+    hidden,
+    out_gate,
+    w_out,
+):
+    caption_count, slots, features = captions.shape
+    images, patches, width = queries.shape
+    packed = 2 * width + HEAD
+    smem = pl.BlockSpec(memory_space=pltpu.SMEM)
+    vmem = pl.BlockSpec(memory_space=pltpu.VMEM)
+    hbm = pl.BlockSpec(memory_space=pl.ANY)
+    dma = pltpu.SemaphoreType.DMA
+    return pl.pallas_call(
+        fused_kernel,
+        out_shape=jax.ShapeDtypeStruct(queries.shape, BF16),
+        in_specs=[smem, smem, vmem, vmem, hbm, hbm, hbm, hbm, hbm, hbm],
+        out_specs=vmem,
+        scratch_shapes=[
+            pltpu.VMEM(captions.shape, BF16),
+            pltpu.VMEM(w_key.shape, BF16),
+            pltpu.VMEM(w_value.shape, BF16),
+            pltpu.VMEM(queries.shape, BF16),
+            pltpu.VMEM(hidden.shape, BF16),
+            pltpu.VMEM((4, w_out.shape[0], width), BF16),
+            pltpu.VMEM(captions.shape, BF16),
+            pltpu.VMEM((caption_count, slots, HEAD), BF16),
+            pltpu.VMEM((images, 2, slots, packed), BF16),
+            pltpu.VMEM((images, 2, slots, packed), BF16),
+            pltpu.VMEM((images, 2, slots, packed), BF16),
+            pltpu.VMEM((images, slots, packed), BF16),
+            pltpu.VMEM((images, 2, slots, 2 * width), BF16),
+            pltpu.VMEM(queries.shape, BF16),
+            pltpu.VMEM((4,) + queries.shape, BF16),
+            pltpu.VMEM(queries.shape, BF16),
+            dma((7,)),
+            dma((images,)), dma((images,)),
+            dma((images,)), dma((images,)),
+            dma((images,)), dma((images,)),
+            dma((2,)), dma((2,)), dma((2,)), dma((2,)),
+            dma((4, images)), dma((4, images)), dma((images,)),
+        ],
+        compiler_params=pltpu.CompilerParams(
+            collective_id=0, has_side_effects=True, vmem_limit_bytes=60 * 1024 * 1024
+        ),
+        cost_estimate=pl.CostEstimate(
+            flops=20_000_000_000, bytes_accessed=20_000_000, transcendentals=1_100_000
+        ),
+    )(
+        image_caption, caption_lengths, t5_gain.reshape(1, -1), out_gate.reshape(images, 1, width),
+        captions, w_key, w_value, queries, hidden, w_out,
+    )
+
+
 def solution(mesh):
     in_specs = (
         P("seq", None, "segment"),
@@ -87,4 +541,6 @@
         P("mp", "seq"),
     )
     out_specs = P("segment", "seq", "mp")
+    fused = (mesh.shape["segment"], mesh.shape["seq"], mesh.shape["mp"]) == (4, 2, 4)
+    shards = fused_shards if fused else general_shards
     return jax.shard_map(shards, mesh=mesh, in_specs=in_specs, out_specs=out_specs, check_vma=False)

time: 405 us -> 208 us (0.51)
  waiting for transfers between devices: 308 us -> 0 us
  Pallas kernels: 0 us -> 203 us
  local copies, waits for them, and re-layouts: 36.7 us -> 4.41 us
  matrix products: 23.3 us -> 0 us
  other arithmetic: 13.6 us -> 0 us
  between operations: 13.3 us -> 0.01 us
  blocking collectives: 6.9 us -> 0 us
    pallas_call x0 -> x1, Pallas kernels: none -> 203 us  [fused_shards(): pl.pallas_call(fused_kernel, out_shape=jax.ShapeDtypeStruct(queries.shape...]
    reduce_scatter x2 -> x0, waiting for transfers between devices: 190 us -> none  [the longest x1 145 us: shards(): lax.psum_scatter(partial_value.astype(jnp.bfloat16), 'mp', scatter_dimens...]
    all_gather x2 -> x0, waiting for transfers between devices: 117 us -> none  [the longest x1 64.9 us: shards(): lax.all_gather(w_out, 'seq', axis=1, tiled=True)]
    dot_general x5 -> x0, matrix products: 23.3 us -> none  [the longest x1 14.2 us: shards(): jnp.dot(attended, lax.all_gather(w_out, 'seq', axis=1, tiled=True), prefe...]
    reshape x2 -> x1, local copies, waits for them, and re-layouts: 14.9 us -> 1.33 us  [fused_shards(): out_gate.reshape(images, 1, width)]
    transpose x1 -> x0, local copies, waits for them, and re-layouts: 12.4 us -> none  [shards(): pieces.transpose(1, 2, 0, 3)]
    psum x1 -> x0, blocking collectives: 6.9 us -> none  [shards(): lax.psum(jnp.sum(caption_values * caption_values, axis=2), 'segment')]
    convert_element_type x2 -> x0, other arithmetic: 6.87 us -> none  [the longest x1 4.73 us: shards(): return result_rows.astype(jnp.bfloat16)]
  transfers between devices with their start and end apart: 4 -> 0, of which waited for: 4 -> 0; matrix products, arithmetic and copies ran while one was open for 10% -> 0% of each run, Pallas kernels for 0% -> 0%
where the time goes in v1:
time: 208 us
  Pallas kernels  203 us (98%)
  local copies, waits for them, and re-layouts  4.41 us (2%)
    pallas_call x1, Pallas kernels, fused_shards(): pl.pallas_call(fused_kernel, out_shape=jax.ShapeDtypeStruct(queries.shape...  203 us

profile of v1, /device:TPU:12, one launch (start us, length us, event | category | flops | bytes accessed | tf_op | source)
XLA Modules:
  0.0 207.6 jit_solution(6732775261049370820)
XLA Ops:
  0.0 1.3 reshape.7.gate
  1.3 203.2 %shard_map.100 = bf16[4,256,1024]{2,1,0:T(8,128)(2,1)} custom-call(s32[16]{0:T(128)} %image_caption.1, s32[16]{0:T(128)} %caption_lengths.1, f32[1,1024]{1,0:T(1,128)} %bitcast.1, f32[4,1,1024]{2,1,0:T(1,128)} %reshape.7.gate, bf16[8,128,1024]{2,1,0:T(8,128)(2,1)} %captions.1, bf16[1024,1024]{1,0:T(8,128)(2,1)} %w_key.1, bf16[1024,1024]{1,0:T(8,128)(2,1)} %w_value.1, ...), custom_call_target="tpu_custom_call" | custom-call | flops 20000000000 | bytes 20000000 | tf_op jit(solution)/shard_map/pallas_call | solution.py:489
  204.5 3.1 %copy.12 = bf16[4,256,1024]{2,1,0:T(8,128)(2,1)} copy(bf16[4,256,1024]{2,1,0:T(8,128)(2,1)} %shard_map.100) | data formatting | bytes 4194304

commit v2 on v1

--- a/solution.py
+++ b/solution.py
@@ -83,10 +83,11 @@
 def fused_kernel(
     image_caption, caption_lengths, gain, gate, captions, w_key, w_value, queries, hidden, w_out,
     result,
-    cap_raw, key_w, value_w, query_v, hidden_v, out_w, scaled, squares,
-    pair_send, pair_recv, own, cross_recv, rows, attended, moving, from_right,
+    cap_raw, kv_w, query_v, out_w, scaled, squares,
+    pair_send, pair_recv, own, cross_recv, rows, attended, moving, from_right, end_rows, end_w,
     local_sem, pair_ssem, pair_rsem, cross_ssem, cross_rsem, row_ssem, row_rsem,
     w_ssem, w_rsem, wf_ssem, wf_rsem, z_ssem, z_rsem, left_rsem,
+    end_ssem, end_rsem, ew_ssem, ew_rsem, ewf_ssem, ewf_rsem,
 ):
     seg = lax.axis_index("segment")
     seq = lax.axis_index("seq")
@@ -97,7 +98,7 @@
     seq_id = {"seq": 1 - seq}
     caption_count, slots, features = cap_raw.shape
     images, patches, width = query_v.shape
-    both = 2 * width
+    rounds = 2 * images
     head_count = width // HEAD
     half = out_w.shape[1] // 2
     total_features = 4 * features
@@ -107,8 +108,8 @@
 
     loads = [
         pltpu.make_async_copy(captions, cap_raw, local_sem.at[0]),
-        pltpu.make_async_copy(w_key, key_w, local_sem.at[1]),
-        pltpu.make_async_copy(w_value, value_w, local_sem.at[2]),
+        pltpu.make_async_copy(w_key, kv_w.at[0], local_sem.at[1]),
+        pltpu.make_async_copy(w_value, kv_w.at[1], local_sem.at[2]),
         pltpu.make_async_copy(queries, query_v, local_sem.at[3]),
         pltpu.make_async_copy(
             w_out.at[:, pl.ds(0, width)], out_w.at[2 * seq], local_sem.at[4]
@@ -116,8 +117,8 @@
         pltpu.make_async_copy(
             w_out.at[:, pl.ds(width, width)], out_w.at[2 * seq + 1], local_sem.at[5]
         ),
-        pltpu.make_async_copy(hidden, hidden_v, local_sem.at[6]),
     ]
+    hidden_load = pltpu.make_async_copy(hidden, query_v, local_sem.at[6])
     for load in loads:
         load.start()
 
@@ -162,7 +163,54 @@
             device_id_type=MESH,
         )
 
+    is_end = (mp == 0) | (mp == 3)
+    first = jnp.where(mp < 2, 3, 0)
+    third = 1 + seq
+    late = 2 - seq
+    inward = jnp.where(mp < 2, 1, 2)
+    owns_first = (first // 2) == seq
+
+    def end_w_direct(step):
+        local_block = seq if step == 0 else 1 - seq
+        return pltpu.make_async_remote_copy(
+            src_ref=w_out.at[half_rows, pl.ds(pl.multiple_of(local_block * width, width), width)],
+            dst_ref=end_w.at[step, half_rows],
+            send_sem=ew_ssem.at[step], recv_sem=ew_rsem.at[step],
+            device_id=device({"mp": inward}), device_id_type=MESH,
+        )
+
+    def end_w_received():
+        return pltpu.make_async_remote_copy(
+            src_ref=out_w.at[first, half_rows],
+            dst_ref=end_w.at[0, half_rows],
+            send_sem=ew_ssem.at[0], recv_sem=ew_rsem.at[0],
+            device_id=device({"mp": inward}), device_id_type=MESH,
+        )
+
+    def end_w_forward(step):
+        return pltpu.make_async_remote_copy(
+            src_ref=end_w.at[step, half_rows],
+            dst_ref=end_w.at[step, half_rows],
+            send_sem=ewf_ssem.at[step], recv_sem=ewf_rsem.at[step],
+            device_id=device(pair_id), device_id_type=MESH,
+        )
+
+    def end_copy(j):
+        return pltpu.make_async_remote_copy(
+            src_ref=attended.at[j], dst_ref=end_rows.at[j],
+            send_sem=end_ssem.at[j], recv_sem=end_rsem.at[j],
+            device_id=device({"mp": inward}), device_id_type=MESH,
+        )
+
     w_copy(0).start()
+
+    @pl.when(is_end)
+    def _():
+        @pl.when(owns_first)
+        def _():
+            end_w_direct(0).start()
+
+        end_w_direct(1).start()
 
     loads[0].wait()
 
@@ -180,22 +228,20 @@
     loads[2].wait()
     tile = 256
 
-    def slot_partial(j, out_core, dst):
-        ids = [image_caption[4 * (2 * x + out_core) + j] % caption_count for x in range(2)]
+    def slot_partial(u, out_core, dst):
+        ids = [image_caption[4 * (2 * x + out_core) + u // 2] % caption_count for x in range(2)]
         lhs = jnp.concatenate([scaled[i] for i in ids], axis=0)
+        half_index = u % 2
 
         @pl.loop(0, width // tile)
         def _(t):
             cols = pl.ds(pl.multiple_of(t * tile, tile), tile)
-            vcols = pl.ds(pl.multiple_of(width + t * tile, tile), tile)
-            k = jnp.dot(lhs, key_w[:, cols], preferred_element_type=F32).astype(BF16)
-            v = jnp.dot(lhs, value_w[:, cols], preferred_element_type=F32).astype(BF16)
+            part = jnp.dot(lhs, kv_w[half_index, :, cols], preferred_element_type=F32).astype(BF16)
             for x in range(2):
-                dst[j, x, :, cols] = k[x * slots : (x + 1) * slots]
-                dst[j, x, :, vcols] = v[x * slots : (x + 1) * slots]
+                dst[u, x, :, cols] = part[x * slots : (x + 1) * slots]
 
         for x in range(2):
-            dst[j, x, :, both:] = squares[ids[x]]
+            dst[u, x, :, width:] = squares[ids[x]]
 
     def pair_copy(j):
         return pltpu.make_async_remote_copy(
@@ -231,15 +277,16 @@
 
     def stage_rows(j):
         cross_copy(j).wait_recv()
-        sums = [ref[...].astype(F32) for ref in (
-            own.at[j, chip, :, pl.ds(both, HEAD)],
-            pair_recv.at[j, chip, :, pl.ds(both, HEAD)],
-            cross_recv.at[j, :, pl.ds(both, HEAD)],
-        )]
-        mean = jnp.sum(sums[0] + sums[1] + sums[2], axis=1, keepdims=True) / total_features
+        tail = pl.ds(width, HEAD)
+        mean = jnp.sum(
+            own[j, chip, :, tail].astype(F32)
+            + pair_recv[j, chip, :, tail].astype(F32)
+            + cross_recv[j, :, tail].astype(F32),
+            axis=1, keepdims=True,
+        ) / total_features
         inverse = lax.rsqrt(mean + 1e-06)
 
-        @pl.loop(0, both // tile)
+        @pl.loop(0, width // tile)
         def _(t):
             cols = pl.ds(pl.multiple_of(t * tile, tile), tile)
             value = (
@@ -252,16 +299,20 @@
         row_copy(j).start()
 
     def stage_attend(j):
-        row_copy(j).wait_recv()
+        row_copy(2 * j).wait_recv()
+        row_copy(2 * j + 1).wait_recv()
         caption = image_caption[4 * seg + j]
         from_first = caption < caption_count
         live = caption_lengths[caption]
         mask = lax.broadcasted_iota(jnp.int32, (patches, slots), 1) < live
+
+        def picked(u, cols):
+            return jnp.where(from_first, rows[u, 0, :, cols], rows[u, 1, :, cols])
+
         for h in range(head_count):
             cols = slice(h * HEAD, (h + 1) * HEAD)
-            vcols = slice(width + h * HEAD, width + (h + 1) * HEAD)
             scores = lax.dot_general(
-                query_v[j, :, cols], jnp.where(from_first, rows[j, 0, :, cols], rows[j, 1, :, cols]),
+                query_v[j, :, cols], picked(2 * j, cols),
                 (((1,), (1,)), ((), ())), preferred_element_type=F32,
             ) * HEAD ** (-0.5)
             scores = jnp.where(mask, scores, -1e30)
@@ -269,9 +320,7 @@
             expd = jnp.exp(scores - top)
             weights = (expd / jnp.sum(expd, axis=1, keepdims=True)).astype(BF16)
             attended[j, :, cols] = jnp.dot(
-                weights,
-                jnp.where(from_first, rows[j, 0, :, vcols], rows[j, 1, :, vcols]),
-                preferred_element_type=F32,
+                weights, picked(2 * j + 1, cols), preferred_element_type=F32
             ).astype(BF16)
 
     def up_copy(n, j):
@@ -329,56 +378,87 @@
 
         send_on(n, j)
 
-    def final_step(j):
-        @pl.when(mp > 0)
-        def _():
-            up_copy(mp, j).wait_recv()
-
-        @pl.when(mp < 3)
-        def _():
-            last_copy(mp, j).wait_recv()
-
+    def joint_step(n, step, j):
         @pl.loop(0, width // tile)
         def _(t):
             cols = pl.ds(pl.multiple_of(t * tile, tile), tile)
+            share = jnp.dot(attended[j], out_w[n, :, cols], preferred_element_type=F32)
+            share = share + jnp.dot(end_rows[j], end_w[step, :, cols], preferred_element_type=F32)
+            moving[n, j, :, cols] = share.astype(BF16)
+
+        send_on(n, j)
+
+    from_below = (mp > 0) & jnp.logical_not((mp == 1) & (third == 1))
+    from_above = (mp < 3) & jnp.logical_not((mp == 2) & (third == 2))
+    has_end_term = jnp.logical_not(is_end) & (third == mp)
+
+    def final_step(j):
+        @pl.when(from_below)
+        def _():
+            up_copy(mp, j).wait_recv()
+
+        @pl.when(from_above)
+        def _():
+            last_copy(mp, j).wait_recv()
+
+        def finish(t, terms):
+            cols = pl.ds(pl.multiple_of(t * tile, tile), tile)
             share = jnp.dot(attended[j], out_w[mp, :, cols], preferred_element_type=F32)
-            below = moving[mp, j, :, cols].astype(F32)
-            above = from_right[j, :, cols].astype(F32)
-            share = share + jnp.where(mp > 0, below, 0.0) + jnp.where(mp < 3, above, 0.0)
+            for term in terms:
+                share = share + term(cols)
             result[j, :, cols] = (
-                hidden_v[j, :, cols].astype(F32) + gate[j, :, cols] * share
+                query_v[j, :, cols].astype(F32) + gate[pl.ds(j, 1), cols] * share
             ).astype(BF16)
 
-    is_end = (mp == 0) | (mp == 3)
-    first = jnp.where(mp < 2, 3, 0)
-    third = 1 + seq
-    late = 2 - seq
-    end_order = (first, third)
+        def below(cols):
+            return moving[mp, j, :, cols].astype(F32)
+
+        def above(cols):
+            return from_right[j, :, cols].astype(F32)
+
+        def end_term(cols):
+            return jnp.dot(end_rows[j], end_w[1, :, cols], preferred_element_type=F32)
+
+        for condition, terms in (
+            (mp == 0, (above,)),
+            (mp == 3, (below,)),
+            (has_end_term & (mp == 1), (above, end_term)),
+            (has_end_term & (mp == 2), (below, end_term)),
+            (jnp.logical_not(is_end) & (third != mp), (below, above)),
+        ):
+            @pl.when(condition)
+            def _():
+                pl.loop(0, width // tile)(lambda t: finish(t, terms))
 
     def wait_send(n, j):
         up_copy(n, j).wait_send()
 
-    @pl.loop(0, images + 4)
-    def _(t):
-        @pl.when(t < images)
-        def _():
-            stage_partial(t)
-
-        @pl.when((t >= 1) & (t < images + 1))
-        def _():
-            stage_pair(t - 1)
-
-        @pl.when((t >= 2) & (t < images + 2))
-        def _():
-            stage_rows(t - 2)
-
-        @pl.when(t == images + 1)
+    @pl.loop(0, rounds + 4)
+    def _(u):
+        @pl.when(u < rounds)
+        def _():
+            stage_partial(u)
+
+        @pl.when((u >= 1) & (u < rounds + 1))
+        def _():
+            stage_pair(u - 1)
+
+        @pl.when((u >= 2) & (u < rounds + 2))
+        def _():
+            stage_rows(u - 2)
+
+        @pl.when(u == rounds + 1)
         def _():
             w_copy(1).start()
 
-        @pl.when((t >= 3) & (t < images + 3))
-        def _():
-            j = t - 3
+        @pl.when((u == 3) & is_end & jnp.logical_not(owns_first))
+        def _():
+            w_copy(0).wait_recv()
+            end_w_received().start()
+
+        @pl.when((u >= 4) & (u % 2 == 0))
+        def _():
+            j = (u - 4) // 2
 
             @pl.when(j == 0)
             def _():
@@ -386,50 +466,66 @@
 
             stage_attend(j)
 
+            @pl.when(is_end)
+            def _():
+                end_copy(j).start()
+
+        @pl.when((u >= 5) & (u % 2 == 1))
+        def _():
+            j = (u - 5) // 2
+
             @pl.when(j == 0)
             def _():
-                w_copy(0).wait_recv()
+                @pl.when(jnp.logical_not(is_end & jnp.logical_not(owns_first)))
+                def _():
+                    w_copy(0).wait_recv()
+
                 w_forward(0).start()
                 loads[4].wait()
                 loads[5].wait()
+
+                @pl.when(jnp.logical_not(is_end))
+                def _():
+                    for step in range(2):
+                        end_w_direct(step).wait_recv()
+                        end_w_forward(step).start()
+
+                    for step in range(2):
+                        end_w_forward(step).wait_recv()
+
                 w_forward(0).wait_recv()
 
-            @pl.when(is_end)
-            def _():
-                for n in end_order:
-                    @pl.when(j >= 1)
-                    def _():
-                        wait_send(n, j - 1)
-
-                    source_step(n, j)
-
-        @pl.when((t >= 4) & jnp.logical_not(is_end))
-        def _():
-            j = t - 4
-            relay_step(first, j)
-            relay_step(3 - first, j)
-
-            @pl.when(third != mp)
-            def _():
-                relay_step(third, j)
+            @pl.when(jnp.logical_not(is_end))
+            def _():
+                end_copy(j).wait_recv()
+                joint_step(first, 0, j)
+
+                @pl.when(third != mp)
+                def _():
+                    joint_step(third, 1, j)
+
+                @pl.when(j >= 1)
+                def _():
+                    relay_step(3 - first, j - 1)
+
+    hidden_load.start()
+
+    @pl.when(jnp.logical_not(is_end))
+    def _():
+        relay_step(3 - first, images - 1)
 
     w_copy(1).wait_recv()
     w_forward(1).start()
     w_forward(1).wait_recv()
-    loads[6].wait()
+    hidden_load.wait()
 
     @pl.loop(0, images)
     def _(j):
         @pl.when(is_end)
         def _():
-            @pl.when(j == 0)
-            def _():
-                for n in end_order:
-                    wait_send(n, images - 1)
-
-            @pl.when(j >= 1)
-            def _():
-                wait_send(late, j - 1)
+            @pl.when(j >= 2)
+            def _():
+                wait_send(late, j - 2)
 
             source_step(late, j)
 
@@ -443,14 +539,30 @@
         w_copy(step).wait_send()
         w_forward(step).wait_send()
 
-    @pl.loop(0, images)
-    def _(j):
-        pair_copy(j).wait_send()
-        cross_copy(j).wait_send()
-        row_copy(j).wait_send()
-
-        @pl.when(jnp.logical_not(is_end))
-        def _():
+    @pl.loop(0, rounds)
+    def _(u):
+        pair_copy(u).wait_send()
+        cross_copy(u).wait_send()
+        row_copy(u).wait_send()
+
+    @pl.when(is_end)
+    def _():
+        for step in range(2):
+            end_w_direct(step).wait_send()
+
+        for j in range(images):
+            end_copy(j).wait_send()
+
+        wait_send(late, images - 2)
+        wait_send(late, images - 1)
+
+    @pl.when(jnp.logical_not(is_end))
+    def _():
+        for step in range(2):
+            end_w_forward(step).wait_send()
+
+        @pl.loop(0, images)
+        def _(j):
             wait_send(first, j)
             wait_send(3 - first, j)
 
@@ -461,10 +573,6 @@
             @pl.when(late != mp)
             def _():
                 wait_send(late, j)
-
-    @pl.when(is_end)
-    def _():
-        wait_send(late, images - 1)
 
 
 def fused_shards(
@@ -481,7 +589,8 @@
 ):
     caption_count, slots, features = captions.shape
     images, patches, width = queries.shape
-    packed = 2 * width + HEAD
+    packed = width + HEAD
+    rounds = 2 * images
     smem = pl.BlockSpec(memory_space=pltpu.SMEM)
     vmem = pl.BlockSpec(memory_space=pltpu.VMEM)
     hbm = pl.BlockSpec(memory_space=pl.ANY)
@@ -493,27 +602,29 @@
         out_specs=vmem,
         scratch_shapes=[
             pltpu.VMEM(captions.shape, BF16),
-            pltpu.VMEM(w_key.shape, BF16),
-            pltpu.VMEM(w_value.shape, BF16),
+            pltpu.VMEM((2,) + w_key.shape, BF16),
             pltpu.VMEM(queries.shape, BF16),
-            pltpu.VMEM(hidden.shape, BF16),
             pltpu.VMEM((4, w_out.shape[0], width), BF16),
             pltpu.VMEM(captions.shape, BF16),
             pltpu.VMEM((caption_count, slots, HEAD), BF16),
-            pltpu.VMEM((images, 2, slots, packed), BF16),
-            pltpu.VMEM((images, 2, slots, packed), BF16),
-            pltpu.VMEM((images, 2, slots, packed), BF16),
-            pltpu.VMEM((images, slots, packed), BF16),
-            pltpu.VMEM((images, 2, slots, 2 * width), BF16),
+            pltpu.VMEM((rounds, 2, slots, packed), BF16),
+            pltpu.VMEM((rounds, 2, slots, packed), BF16),
+            pltpu.VMEM((rounds, 2, slots, packed), BF16),
+            pltpu.VMEM((rounds, slots, packed), BF16),
+            pltpu.VMEM((rounds, 2, slots, width), BF16),
             pltpu.VMEM(queries.shape, BF16),
             pltpu.VMEM((4,) + queries.shape, BF16),
             pltpu.VMEM(queries.shape, BF16),
+            pltpu.VMEM(queries.shape, BF16),
+            pltpu.VMEM((2, w_out.shape[0], width), BF16),
             dma((7,)),
-            dma((images,)), dma((images,)),
-            dma((images,)), dma((images,)),
+            dma((rounds,)), dma((rounds,)),
+            dma((rounds,)), dma((rounds,)),
+            dma((rounds,)), dma((rounds,)),
+            dma((2,)), dma((2,)), dma((2,)), dma((2,)),
+            dma((4, images)), dma((4, images)), dma((images,)),
             dma((images,)), dma((images,)),
             dma((2,)), dma((2,)), dma((2,)), dma((2,)),
-            dma((4, images)), dma((4, images)), dma((images,)),
         ],
         compiler_params=pltpu.CompilerParams(
             collective_id=0, has_side_effects=True, vmem_limit_bytes=60 * 1024 * 1024
@@ -522,7 +633,7 @@
             flops=20_000_000_000, bytes_accessed=20_000_000, transcendentals=1_100_000
         ),
     )(
-        image_caption, caption_lengths, t5_gain.reshape(1, -1), out_gate.reshape(images, 1, width),
+        image_caption, caption_lengths, t5_gain.reshape(1, -1), out_gate,
         captions, w_key, w_value, queries, hidden, w_out,
     )
 

time: 208 us -> 202 us (0.971); the launches traced: 208 us -> 199 us
  Pallas kernels: 203 us -> 196 us
    pallas_call x1, Pallas kernels: 203 us -> 196 us  [fused_shards(): pl.pallas_call(fused_kernel, out_shape=jax.ShapeDtypeStruct(queries.shape...]
where the time goes in v2:
time: 202 us; the launch traced here: 199 us
  Pallas kernels  196 us (97%)
  local copies, waits for them, and re-layouts  3.08 us (2%)
    pallas_call x1, Pallas kernels, fused_shards(): pl.pallas_call(fused_kernel, out_shape=jax.ShapeDtypeStruct(queries.shape...  196 us

profile of v2, /device:TPU:12, one launch (start us, length us, event | category | flops | bytes accessed | tf_op | source)
XLA Modules:
  0.0 199.0 jit_solution(11312559932134132109)
XLA Ops:
  0.0 195.9 %shard_map.100 = bf16[4,256,1024]{2,1,0:T(8,128)(2,1)} custom-call(s32[16]{0:T(128)} %image_caption.1, s32[16]{0:T(128)} %caption_lengths.1, f32[1,1024]{1,0:T(1,128)} %bitcast.1, f32[4,1024]{1,0:T(4,128)} %gate.1, bf16[8,128,1024]{2,1,0:T(8,128)(2,1)} %captions.1, bf16[1024,1024]{1,0:T(8,128)(2,1)} %w_key.1, bf16[1024,1024]{1,0:T(8,128)(2,1)} %w_value.1, ...), custom_call_target="tpu_custom_call" | custom-call | flops 20000000000 | bytes 20000000 | tf_op jit(solution)/shard_map/pallas_call | solution.py:598
  195.9 3.1 %copy.12 = bf16[4,256,1024]{2,1,0:T(8,128)(2,1)} copy(bf16[4,256,1024]{2,1,0:T(8,128)(2,1)} %shard_map.100) | data formatting | bytes 4194304

commit v3 on v2

--- a/solution.py
+++ b/solution.py
@@ -86,8 +86,8 @@
     cap_raw, kv_w, query_v, out_w, scaled, squares,
     pair_send, pair_recv, own, cross_recv, rows, attended, moving, from_right, end_rows, end_w,
     local_sem, pair_ssem, pair_rsem, cross_ssem, cross_rsem, row_ssem, row_rsem,
-    w_ssem, w_rsem, wf_ssem, wf_rsem, z_ssem, z_rsem, left_rsem,
-    end_ssem, end_rsem, ew_ssem, ew_rsem, ewf_ssem, ewf_rsem,
+    w_ssem, w_rsem, z_ssem, z_rsem, left_rsem,
+    end_ssem, end_rsem, ew_ssem, ew_rsem, wx_ssem, wx_rsem, wp_ssem, wp_rsem,
 ):
     seg = lax.axis_index("segment")
     seq = lax.axis_index("seq")
@@ -100,7 +100,7 @@
     images, patches, width = query_v.shape
     rounds = 2 * images
     head_count = width // HEAD
-    half = out_w.shape[1] // 2
+    quarter = out_w.shape[1] // 4
     total_features = 4 * features
 
     def device(ids):
@@ -137,29 +137,21 @@
     neighbours = 5 - (mp == 0).astype(jnp.int32) - (mp == 3).astype(jnp.int32)
     pl.semaphore_wait(barrier, neighbours)
 
-    half_rows = pl.ds(pl.multiple_of(core * half, half), half)
+    def quarter_of(owner):
+        return pl.ds(pl.multiple_of(owner * quarter, quarter), quarter)
+
+    near_rows = quarter_of(seg)
+    far_rows = quarter_of((seg + 2) % 4)
 
     def w_copy(step):
         local_block = seq if step == 0 else 1 - seq
         block = 2 * seq + local_block
         return pltpu.make_async_remote_copy(
-            src_ref=w_out.at[half_rows, pl.ds(pl.multiple_of(local_block * width, width), width)],
-            dst_ref=out_w.at[block, half_rows],
+            src_ref=w_out.at[near_rows, pl.ds(pl.multiple_of(local_block * width, width), width)],
+            dst_ref=out_w.at[block, near_rows],
             send_sem=w_ssem.at[step],
             recv_sem=w_rsem.at[step],
             device_id=device(seq_id),
-            device_id_type=MESH,
-        )
-
-    def w_forward(step):
-        other = 1 - seq
-        block = 2 * other + (other if step == 0 else 1 - other)
-        return pltpu.make_async_remote_copy(
-            src_ref=out_w.at[block, half_rows],
-            dst_ref=out_w.at[block, half_rows],
-            send_sem=wf_ssem.at[step],
-            recv_sem=wf_rsem.at[step],
-            device_id=device(pair_id),
             device_id_type=MESH,
         )
 
@@ -173,27 +165,62 @@
     def end_w_direct(step):
         local_block = seq if step == 0 else 1 - seq
         return pltpu.make_async_remote_copy(
-            src_ref=w_out.at[half_rows, pl.ds(pl.multiple_of(local_block * width, width), width)],
-            dst_ref=end_w.at[step, half_rows],
+            src_ref=w_out.at[near_rows, pl.ds(pl.multiple_of(local_block * width, width), width)],
+            dst_ref=end_w.at[step, near_rows],
             send_sem=ew_ssem.at[step], recv_sem=ew_rsem.at[step],
             device_id=device({"mp": inward}), device_id_type=MESH,
         )
 
     def end_w_received():
         return pltpu.make_async_remote_copy(
-            src_ref=out_w.at[first, half_rows],
-            dst_ref=end_w.at[0, half_rows],
+            src_ref=out_w.at[first, near_rows],
+            dst_ref=end_w.at[0, near_rows],
             send_sem=ew_ssem.at[0], recv_sem=ew_rsem.at[0],
             device_id=device({"mp": inward}), device_id_type=MESH,
         )
 
-    def end_w_forward(step):
-        return pltpu.make_async_remote_copy(
-            src_ref=end_w.at[step, half_rows],
-            dst_ref=end_w.at[step, half_rows],
-            send_sem=ewf_ssem.at[step], recv_sem=ewf_rsem.at[step],
+    other = 1 - seq
+    blocks = (
+        out_w.at[2 * other + other],
+        out_w.at[2 * other + 1 - other],
+        end_w.at[0],
+        end_w.at[1],
+    )
+
+    def cross_spread(b):
+        return pltpu.make_async_remote_copy(
+            src_ref=blocks[b].at[near_rows], dst_ref=blocks[b].at[near_rows],
+            send_sem=wx_ssem.at[b], recv_sem=wx_rsem.at[b],
+            device_id=device(cross_id), device_id_type=MESH,
+        )
+
+    def pair_spread(b, i):
+        part = far_rows if i else near_rows
+        return pltpu.make_async_remote_copy(
+            src_ref=blocks[b].at[part], dst_ref=blocks[b].at[part],
+            send_sem=wp_ssem.at[b, i], recv_sem=wp_rsem.at[b, i],
             device_id=device(pair_id), device_id_type=MESH,
         )
+
+    def spread_start(b):
+        cross_spread(b).start()
+        pair_spread(b, 0).start()
+
+    def spread_far(b):
+        cross_spread(b).wait_recv()
+        pair_spread(b, 1).start()
+
+    def spread_end(b):
+        pair_spread(b, 0).wait_recv()
+        pair_spread(b, 1).wait_recv()
+
+    def spread_sent(b):
+        cross_spread(b).wait_send()
+        pair_spread(b, 0).wait_send()
+        pair_spread(b, 1).wait_send()
+
+    inner = jnp.logical_not(is_end)
+    spreads_first = jnp.logical_not(is_end & jnp.logical_not(owns_first))
 
     def end_copy(j):
         return pltpu.make_async_remote_copy(
@@ -433,7 +460,7 @@
     def wait_send(n, j):
         up_copy(n, j).wait_send()
 
-    @pl.loop(0, rounds + 4)
+    @pl.loop(0, rounds + 6)
     def _(u):
         @pl.when(u < rounds)
         def _():
@@ -447,16 +474,17 @@
         def _():
             stage_rows(u - 2)
 
-        @pl.when(u == rounds + 1)
-        def _():
-            w_copy(1).start()
-
-        @pl.when((u == 3) & is_end & jnp.logical_not(owns_first))
+        @pl.when((u == 2) & is_end & jnp.logical_not(owns_first))
         def _():
             w_copy(0).wait_recv()
             end_w_received().start()
 
-        @pl.when((u >= 4) & (u % 2 == 0))
+        @pl.when((u == 3) & spreads_first)
+        def _():
+            w_copy(0).wait_recv()
+            spread_start(0)
+
+        @pl.when((u >= 4) & (u % 2 == 0) & (u < rounds + 4))
         def _():
             j = (u - 4) // 2
 
@@ -470,35 +498,65 @@
             def _():
                 end_copy(j).start()
 
-        @pl.when((u >= 5) & (u % 2 == 1))
-        def _():
-            j = (u - 5) // 2
+        @pl.when(u == 4)
+        def _():
+            w_copy(1).start()
+
+            @pl.when(inner)
+            def _():
+                end_w_direct(0).wait_recv()
+                spread_start(2)
+
+        @pl.when(u == 5)
+        def _():
+            @pl.when(spreads_first)
+            def _():
+                spread_far(0)
+
+            @pl.when(inner)
+            def _():
+                end_w_direct(1).wait_recv()
+                spread_start(3)
+
+        @pl.when((u == 6) & inner)
+        def _():
+            spread_far(2)
+
+        @pl.when(u == 8)
+        def _():
+            w_copy(1).wait_recv()
+            spread_start(1)
+
+        @pl.when(u == 10)
+        def _():
+            spread_far(1)
+
+        @pl.when((u >= 7) & (u % 2 == 1))
+        def _():
+            j = (u - 7) // 2
 
             @pl.when(j == 0)
             def _():
-                @pl.when(jnp.logical_not(is_end & jnp.logical_not(owns_first)))
-                def _():
-                    w_copy(0).wait_recv()
-
-                w_forward(0).start()
                 loads[4].wait()
                 loads[5].wait()
 
-                @pl.when(jnp.logical_not(is_end))
+                @pl.when(spreads_first)
                 def _():
-                    for step in range(2):
-                        end_w_direct(step).wait_recv()
-                        end_w_forward(step).start()
-
-                    for step in range(2):
-                        end_w_forward(step).wait_recv()
-
-                w_forward(0).wait_recv()
-
-            @pl.when(jnp.logical_not(is_end))
+                    spread_end(0)
+
+                @pl.when(inner)
+                def _():
+                    spread_far(3)
+                    spread_end(2)
+
+            @pl.when(inner)
             def _():
                 end_copy(j).wait_recv()
                 joint_step(first, 0, j)
+
+                @pl.when(j == 0)
+                def _():
+                    spread_end(3)
 
                 @pl.when(third != mp)
                 def _():
@@ -514,9 +572,7 @@
     def _():
         relay_step(3 - first, images - 1)
 
-    w_copy(1).wait_recv()
-    w_forward(1).start()
-    w_forward(1).wait_recv()
+    spread_end(1)
     hidden_load.wait()
 
     @pl.loop(0, images)
@@ -537,7 +593,12 @@
 
     for step in range(2):
         w_copy(step).wait_send()
-        w_forward(step).wait_send()
+
+    spread_sent(1)
+
+    @pl.when(spreads_first)
+    def _():
+        spread_sent(0)
 
     @pl.loop(0, rounds)
     def _(u):
@@ -559,7 +620,7 @@
     @pl.when(jnp.logical_not(is_end))
     def _():
         for step in range(2):
-            end_w_forward(step).wait_send()
+            spread_sent(2 + step)
 
         @pl.loop(0, images)
         def _(j):
@@ -621,10 +682,11 @@
             dma((rounds,)), dma((rounds,)),
             dma((rounds,)), dma((rounds,)),
             dma((rounds,)), dma((rounds,)),
-            dma((2,)), dma((2,)), dma((2,)), dma((2,)),
+            dma((2,)), dma((2,)),
             dma((4, images)), dma((4, images)), dma((images,)),
             dma((images,)), dma((images,)),
-            dma((2,)), dma((2,)), dma((2,)), dma((2,)),
+            dma((2,)), dma((2,)),
+            dma((4,)), dma((4,)), dma((4, 2)), dma((4, 2)),
         ],
         compiler_params=pltpu.CompilerParams(
             collective_id=0, has_side_effects=True, vmem_limit_bytes=60 * 1024 * 1024

time: 202 us -> 219 us (1.084); the launches traced: 199 us -> 219 us
  Pallas kernels: 196 us -> 216 us
    pallas_call x1, Pallas kernels: 196 us -> 216 us  [fused_shards(): pl.pallas_call(fused_kernel, out_shape=jax.ShapeDtypeStruct(queries.shape...]
where the time goes in v3:
time: 219 us
  Pallas kernels  216 us (99%)
  local copies, waits for them, and re-layouts  3.08 us (1%)
    pallas_call x1, Pallas kernels, fused_shards(): pl.pallas_call(fused_kernel, out_shape=jax.ShapeDtypeStruct(queries.shape...  216 us

profile of v3, /device:TPU:12, one launch (start us, length us, event | category | flops | bytes accessed | tf_op | source)
XLA Modules:
  0.0 219.2 jit_solution(10451466660110537477)
XLA Ops:
  0.0 216.1 %shard_map.100 = bf16[4,256,1024]{2,1,0:T(8,128)(2,1)} custom-call(s32[16]{0:T(128)} %image_caption.1, s32[16]{0:T(128)} %caption_lengths.1, f32[1,1024]{1,0:T(1,128)} %bitcast.1, f32[4,1024]{1,0:T(4,128)} %gate.1, bf16[8,128,1024]{2,1,0:T(8,128)(2,1)} %captions.1, bf16[1024,1024]{1,0:T(8,128)(2,1)} %w_key.1, bf16[1024,1024]{1,0:T(8,128)(2,1)} %w_value.1, ...), custom_call_target="tpu_custom_call" | custom-call | flops 20000000000 | bytes 20000000 | tf_op jit(solution)/shard_map/pallas_call | solution.py:659
  216.1 3.1 %copy.12 = bf16[4,256,1024]{2,1,0:T(8,128)(2,1)} copy(bf16[4,256,1024]{2,1,0:T(8,128)(2,1)} %shard_map.100) | data formatting | bytes 4194304

commit v4 on v3

--- a/solution.py
+++ b/solution.py
@@ -137,18 +137,20 @@
     neighbours = 5 - (mp == 0).astype(jnp.int32) - (mp == 3).astype(jnp.int32)
     pl.semaphore_wait(barrier, neighbours)
 
-    def quarter_of(owner):
-        return pl.ds(pl.multiple_of(owner * quarter, quarter), quarter)
-
-    near_rows = quarter_of(seg)
-    far_rows = quarter_of((seg + 2) % 4)
+    def part_of(owner, size):
+        return pl.ds(pl.multiple_of(owner * size, size), size)
+
+    half_rows = part_of(core, 2 * quarter)
+    near_rows = part_of(seg, quarter)
+    far_rows = part_of((seg + 2) % 4, quarter)
+    rows_of_step = (half_rows, near_rows)
 
     def w_copy(step):
         local_block = seq if step == 0 else 1 - seq
         block = 2 * seq + local_block
         return pltpu.make_async_remote_copy(
-            src_ref=w_out.at[near_rows, pl.ds(pl.multiple_of(local_block * width, width), width)],
-            dst_ref=out_w.at[block, near_rows],
+            src_ref=w_out.at[rows_of_step[step], pl.ds(pl.multiple_of(local_block * width, width), width)],
+            dst_ref=out_w.at[block, rows_of_step[step]],
             send_sem=w_ssem.at[step],
             recv_sem=w_rsem.at[step],
             device_id=device(seq_id),
@@ -165,16 +167,16 @@
     def end_w_direct(step):
         local_block = seq if step == 0 else 1 - seq
         return pltpu.make_async_remote_copy(
-            src_ref=w_out.at[near_rows, pl.ds(pl.multiple_of(local_block * width, width), width)],
-            dst_ref=end_w.at[step, near_rows],
+            src_ref=w_out.at[rows_of_step[step], pl.ds(pl.multiple_of(local_block * width, width), width)],
+            dst_ref=end_w.at[step, rows_of_step[step]],
             send_sem=ew_ssem.at[step], recv_sem=ew_rsem.at[step],
             device_id=device({"mp": inward}), device_id_type=MESH,
         )
 
     def end_w_received():
         return pltpu.make_async_remote_copy(
-            src_ref=out_w.at[first, near_rows],
-            dst_ref=end_w.at[0, near_rows],
+            src_ref=out_w.at[first, half_rows],
+            dst_ref=end_w.at[0, half_rows],
             send_sem=ew_ssem.at[0], recv_sem=ew_rsem.at[0],
             device_id=device({"mp": inward}), device_id_type=MESH,
         )
@@ -195,7 +197,7 @@
         )
 
     def pair_spread(b, i):
-        part = far_rows if i else near_rows
+        part = far_rows if i else (near_rows if b % 2 else half_rows)
         return pltpu.make_async_remote_copy(
             src_ref=blocks[b].at[part], dst_ref=blocks[b].at[part],
             send_sem=wp_ssem.at[b, i], recv_sem=wp_rsem.at[b, i],
@@ -203,7 +205,8 @@
         )
 
     def spread_start(b):
-        cross_spread(b).start()
+        if b % 2:
+            cross_spread(b).start()
         pair_spread(b, 0).start()
 
     def spread_far(b):
@@ -212,12 +215,14 @@
 
     def spread_end(b):
         pair_spread(b, 0).wait_recv()
-        pair_spread(b, 1).wait_recv()
+        if b % 2:
+            pair_spread(b, 1).wait_recv()
 
     def spread_sent(b):
-        cross_spread(b).wait_send()
         pair_spread(b, 0).wait_send()
-        pair_spread(b, 1).wait_send()
+        if b % 2:
+            cross_spread(b).wait_send()
+            pair_spread(b, 1).wait_send()
 
     inner = jnp.logical_not(is_end)
     spreads_first = jnp.logical_not(is_end & jnp.logical_not(owns_first))
@@ -460,7 +465,7 @@
     def wait_send(n, j):
         up_copy(n, j).wait_send()
 
-    @pl.loop(0, rounds + 6)
+    @pl.loop(0, rounds + 4)
     def _(u):
         @pl.when(u < rounds)
         def _():
@@ -474,17 +479,12 @@
         def _():
             stage_rows(u - 2)
 
-        @pl.when((u == 2) & is_end & jnp.logical_not(owns_first))
+        @pl.when((u == 3) & is_end & jnp.logical_not(owns_first))
         def _():
             w_copy(0).wait_recv()
             end_w_received().start()
 
-        @pl.when((u == 3) & spreads_first)
-        def _():
-            w_copy(0).wait_recv()
-            spread_start(0)
-
-        @pl.when((u >= 4) & (u % 2 == 0) & (u < rounds + 4))
+        @pl.when((u >= 4) & (u % 2 == 0))
         def _():
             j = (u - 4) // 2
 
@@ -500,95 +500,94 @@
 
         @pl.when(u == 4)
         def _():
+            @pl.when(spreads_first)
+            def _():
+                w_copy(0).wait_recv()
+                spread_start(0)
+
+            @pl.when(inner)
+            def _():
+                end_w_direct(1).wait_recv()
+                spread_start(3)
+
+        @pl.when(u == 8)
+        def _():
+            w_copy(1).wait_recv()
+            spread_start(1)
+
+        @pl.when(u == 10)
+        def _():
+            spread_far(1)
+
+        @pl.when(u == 5)
+        def _():
             w_copy(1).start()
+            loads[4].wait()
+            loads[5].wait()
+
+            @pl.when(spreads_first)
+            def _():
+                spread_end(0)
 
             @pl.when(inner)
             def _():
+                spread_far(3)
                 end_w_direct(0).wait_recv()
                 spread_start(2)
-
-        @pl.when(u == 5)
-        def _():
-            @pl.when(spreads_first)
-            def _():
-                spread_far(0)
-
-            @pl.when(inner)
-            def _():
-                end_w_direct(1).wait_recv()
-                spread_start(3)
-
-        @pl.when((u == 6) & inner)
-        def _():
-            spread_far(2)
-
-        @pl.when(u == 8)
-        def _():
-            w_copy(1).wait_recv()
-            spread_start(1)
-
-        @pl.when(u == 10)
-        def _():
-            spread_far(1)
-
-        @pl.when((u >= 7) & (u % 2 == 1))
-        def _():
-            j = (u - 7) // 2
+                spread_end(2)
+
+        @pl.when((u >= 5) & (u % 2 == 1) & inner)
+        def _():
+            j = (u - 5) // 2
+            end_copy(j).wait_recv()
+            joint_step(first, 0, j)
 
             @pl.when(j == 0)
             def _():
-                loads[4].wait()
-                loads[5].wait()
-
-                @pl.when(spreads_first)
-                def _():
-                    spread_end(0)
-
-                @pl.when(inner)
-                def _():
-                    spread_far(3)
-                    spread_end(2)
-
-            @pl.when(inner)
-            def _():
-                end_copy(j).wait_recv()
-                joint_step(first, 0, j)
-
-                @pl.when(j == 0)
-                def _():
-                    spread_end(3)
-
-                @pl.when(third != mp)
-                def _():
-                    joint_step(third, 1, j)
-
-                @pl.when(j >= 1)
-                def _():
-                    relay_step(3 - first, j - 1)
+                spread_end(3)
+
+            @pl.when(third != mp)
+            def _():
+                joint_step(third, 1, j)
+
+            @pl.when((j >= 1) & (j < images - 1))
+            def _():
+                relay_step(3 - first, j - 1)
 
     hidden_load.start()
 
-    @pl.when(jnp.logical_not(is_end))
+    spread_end(1)
+
+    @pl.when(is_end)
     def _():
-        relay_step(3 - first, images - 1)
-
-    spread_end(1)
+        @pl.loop(0, images)
+        def _(j):
+            @pl.when(j >= 2)
+            def _():
+                wait_send(late, j - 2)
+
+            source_step(late, j)
+
+    @pl.when(inner)
+    def _():
+        @pl.loop(0, images + 2)
+        def _(t):
+            half_count = images // 2
+            outward = (t == half_count) | (t == images + 1)
+            late_j = t - (t > half_count).astype(jnp.int32)
+
+            @pl.when(outward)
+            def _():
+                relay_step(3 - first, images - 2 + (t > half_count).astype(jnp.int32))
+
+            @pl.when(jnp.logical_not(outward) & (late != mp))
+            def _():
+                relay_step(late, late_j)
+
     hidden_load.wait()
 
     @pl.loop(0, images)
     def _(j):
-        @pl.when(is_end)
-        def _():
-            @pl.when(j >= 2)
-            def _():
-                wait_send(late, j - 2)
-
-            source_step(late, j)
-
-        @pl.when(jnp.logical_not(is_end) & (late != mp))
-        def _():
-            relay_step(late, j)
-
         final_step(j)
 
     for step in range(2):

time: 219 us -> 166 us (0.76)
  Pallas kernels: 216 us -> 162 us
    pallas_call x1, Pallas kernels: 216 us -> 162 us  [fused_shards(): pl.pallas_call(fused_kernel, out_shape=jax.ShapeDtypeStruct(queries.shape...]
where the time goes in v4:
time: 166 us; the launch traced here: 165 us
  Pallas kernels  162 us (98%)
  local copies, waits for them, and re-layouts  3.08 us (2%)
    pallas_call x1, Pallas kernels, fused_shards(): pl.pallas_call(fused_kernel, out_shape=jax.ShapeDtypeStruct(queries.shape...  162 us

profile of v4, /device:TPU:12, one launch (start us, length us, event | category | flops | bytes accessed | tf_op | source)
XLA Modules:
  0.0 164.8 jit_solution(9088752025638284993)
XLA Ops:
  0.0 161.7 %shard_map.100 = bf16[4,256,1024]{2,1,0:T(8,128)(2,1)} custom-call(s32[16]{0:T(128)} %image_caption.1, s32[16]{0:T(128)} %caption_lengths.1, f32[1,1024]{1,0:T(1,128)} %bitcast.1, f32[4,1024]{1,0:T(4,128)} %gate.1, bf16[8,128,1024]{2,1,0:T(8,128)(2,1)} %captions.1, bf16[1024,1024]{1,0:T(8,128)(2,1)} %w_key.1, bf16[1024,1024]{1,0:T(8,128)(2,1)} %w_value.1, ...), custom_call_target="tpu_custom_call" | custom-call | flops 20000000000 | bytes 20000000 | tf_op jit(solution)/shard_map/pallas_call | solution.py:658
  161.7 3.1 %copy.12 = bf16[4,256,1024]{2,1,0:T(8,128)(2,1)} copy(bf16[4,256,1024]{2,1,0:T(8,128)(2,1)} %shard_map.100) | data formatting | bytes 4194304

commit v5 on v4

--- a/solution.py
+++ b/solution.py
@@ -141,8 +141,8 @@
         return pl.ds(pl.multiple_of(owner * size, size), size)
 
     half_rows = part_of(core, 2 * quarter)
-    near_rows = part_of(seg, quarter)
-    far_rows = part_of((seg + 2) % 4, quarter)
+    near_rows = part_of(2 * core + chip, quarter)
+    far_rows = part_of(2 * core + 1 - chip, quarter)
     rows_of_step = (half_rows, near_rows)
 
     def w_copy(step):
@@ -167,16 +167,16 @@
     def end_w_direct(step):
         local_block = seq if step == 0 else 1 - seq
         return pltpu.make_async_remote_copy(
-            src_ref=w_out.at[rows_of_step[step], pl.ds(pl.multiple_of(local_block * width, width), width)],
-            dst_ref=end_w.at[step, rows_of_step[step]],
+            src_ref=w_out.at[near_rows, pl.ds(pl.multiple_of(local_block * width, width), width)],
+            dst_ref=end_w.at[step, near_rows],
             send_sem=ew_ssem.at[step], recv_sem=ew_rsem.at[step],
             device_id=device({"mp": inward}), device_id_type=MESH,
         )
 
     def end_w_received():
         return pltpu.make_async_remote_copy(
-            src_ref=out_w.at[first, half_rows],
-            dst_ref=end_w.at[0, half_rows],
+            src_ref=out_w.at[first, near_rows],
+            dst_ref=end_w.at[0, near_rows],
             send_sem=ew_ssem.at[0], recv_sem=ew_rsem.at[0],
             device_id=device({"mp": inward}), device_id_type=MESH,
         )
@@ -197,7 +197,7 @@
         )
 
     def pair_spread(b, i):
-        part = far_rows if i else (near_rows if b % 2 else half_rows)
+        part = far_rows if i else (near_rows if b else half_rows)
         return pltpu.make_async_remote_copy(
             src_ref=blocks[b].at[part], dst_ref=blocks[b].at[part],
             send_sem=wp_ssem.at[b, i], recv_sem=wp_rsem.at[b, i],
@@ -205,7 +205,7 @@
         )
 
     def spread_start(b):
-        if b % 2:
+        if b:
             cross_spread(b).start()
         pair_spread(b, 0).start()
 
@@ -215,12 +215,12 @@
 
     def spread_end(b):
         pair_spread(b, 0).wait_recv()
-        if b % 2:
+        if b:
             pair_spread(b, 1).wait_recv()
 
     def spread_sent(b):
         pair_spread(b, 0).wait_send()
-        if b % 2:
+        if b:
             cross_spread(b).wait_send()
             pair_spread(b, 1).wait_send()
 
@@ -234,7 +234,9 @@
             device_id=device({"mp": inward}), device_id_type=MESH,
         )
 
-    w_copy(0).start()
+    @pl.when(owns_first)
+    def _():
+        w_copy(0).start()
 
     @pl.when(is_end)
     def _():
@@ -465,76 +467,94 @@
     def wait_send(n, j):
         up_copy(n, j).wait_send()
 
+    near = inner & owns_first
+    distant = inner & jnp.logical_not(owns_first)
+
     @pl.loop(0, rounds + 4)
     def _(u):
-        @pl.when(u < rounds)
+        @pl.when((u >= 1) & (u < rounds + 1))
+        def _():
+            stage_pair(u - 1)
+
+        @pl.when(u < 2)
         def _():
             stage_partial(u)
 
-        @pl.when((u >= 1) & (u < rounds + 1))
-        def _():
-            stage_pair(u - 1)
-
         @pl.when((u >= 2) & (u < rounds + 2))
         def _():
             stage_rows(u - 2)
 
-        @pl.when((u == 3) & is_end & jnp.logical_not(owns_first))
+        @pl.when((u == 3) & jnp.logical_not(owns_first))
+        def _():
+            w_copy(0).start()
+
+            @pl.when(is_end)
+            def _():
+                w_copy(0).wait_recv()
+                end_w_received().start()
+
+        @pl.when((u == 3) & near)
+        def _():
+            end_w_direct(0).wait_recv()
+            spread_start(2)
+
+        @pl.when((u >= 4) & (u % 2 == 0))
+        def _():
+            j = (u - 4) // 2
+
+            @pl.when(j == 0)
+            def _():
+                loads[3].wait()
+
+            stage_attend(j)
+
+            @pl.when(is_end)
+            def _():
+                end_copy(j).start()
+
+        @pl.when((u == 4) & near)
+        def _():
+            spread_far(2)
+            end_w_direct(1).wait_recv()
+            spread_start(3)
+
+        @pl.when((u == 4) & distant)
         def _():
             w_copy(0).wait_recv()
-            end_w_received().start()
-
-        @pl.when((u >= 4) & (u % 2 == 0))
-        def _():
-            j = (u - 4) // 2
-
-            @pl.when(j == 0)
-            def _():
-                loads[3].wait()
-
-            stage_attend(j)
-
-            @pl.when(is_end)
-            def _():
-                end_copy(j).start()
-
-        @pl.when(u == 4)
-        def _():
-            @pl.when(spreads_first)
-            def _():
-                w_copy(0).wait_recv()
-                spread_start(0)
-
-            @pl.when(inner)
-            def _():
-                end_w_direct(1).wait_recv()
-                spread_start(3)
-
-        @pl.when(u == 8)
-        def _():
-            w_copy(1).wait_recv()
-            spread_start(1)
-
-        @pl.when(u == 10)
-        def _():
-            spread_far(1)
+            spread_start(0)
+            end_w_direct(0).wait_recv()
+            spread_start(2)
+
+        @pl.when((u >= 2) & (u < rounds))
+        def _():
+            stage_partial(u)
 
         @pl.when(u == 5)
         def _():
-            w_copy(1).start()
             loads[4].wait()
             loads[5].wait()
 
-            @pl.when(spreads_first)
-            def _():
+            @pl.when(distant)
+            def _():
+                spread_far(2)
                 spread_end(0)
 
             @pl.when(inner)
             def _():
-                spread_far(3)
-                end_w_direct(0).wait_recv()
-                spread_start(2)
                 spread_end(2)
+
+        @pl.when(u == 6)
+        def _():
+            w_copy(1).start()
+
+        @pl.when((u == 7) & distant)
+        def _():
+            end_w_direct(1).wait_recv()
+            spread_start(3)
+
+        @pl.when((u == 9) & distant)
+        def _():
+            spread_far(3)
 
         @pl.when((u >= 5) & (u % 2 == 1) & inner)
         def _():
@@ -542,21 +562,43 @@
             end_copy(j).wait_recv()
             joint_step(first, 0, j)
 
-            @pl.when(j == 0)
-            def _():
+            @pl.when((j == 0) & near)
+            def _():
+                spread_far(3)
                 spread_end(3)
 
-            @pl.when(third != mp)
+            @pl.when(near)
             def _():
                 joint_step(third, 1, j)
 
-            @pl.when((j >= 1) & (j < images - 1))
-            def _():
-                relay_step(3 - first, j - 1)
+        @pl.when((u == 7) & owns_first)
+        def _():
+            w_copy(0).wait_recv()
+            spread_start(0)
+            spread_end(0)
+
+        @pl.when((u == 7) | (u == 9))
+        def _():
+            @pl.when(inner)
+            def _():
+                relay_step(3 - first, (u - 7) // 2)
+
+        @pl.when(u == 9)
+        def _():
+            w_copy(1).wait_recv()
+            spread_start(1)
+
+        @pl.when(u == 11)
+        def _():
+            spread_far(1)
 
     hidden_load.start()
 
     spread_end(1)
+
+    @pl.when(distant)
+    def _():
+        spread_end(3)
 
     @pl.when(is_end)
     def _():

time: 166 us -> 175 us (1.054)
  Pallas kernels: 162 us -> 172 us
    pallas_call x1, Pallas kernels: 162 us -> 172 us  [fused_shards(): pl.pallas_call(fused_kernel, out_shape=jax.ShapeDtypeStruct(queries.shape...]
where the time goes in v5:
time: 175 us
  Pallas kernels  172 us (98%)
  local copies, waits for them, and re-layouts  3.08 us (2%)
    pallas_call x1, Pallas kernels, fused_shards(): pl.pallas_call(fused_kernel, out_shape=jax.ShapeDtypeStruct(queries.shape...  172 us

profile of v5, /device:TPU:12, one launch (start us, length us, event | category | flops | bytes accessed | tf_op | source)
XLA Modules:
  0.0 174.7 jit_solution(1388132868205082166)
XLA Ops:
  0.0 171.6 %shard_map.100 = bf16[4,256,1024]{2,1,0:T(8,128)(2,1)} custom-call(s32[16]{0:T(128)} %image_caption.1, s32[16]{0:T(128)} %caption_lengths.1, f32[1,1024]{1,0:T(1,128)} %bitcast.1, f32[4,1024]{1,0:T(4,128)} %gate.1, bf16[8,128,1024]{2,1,0:T(8,128)(2,1)} %captions.1, bf16[1024,1024]{1,0:T(8,128)(2,1)} %w_key.1, bf16[1024,1024]{1,0:T(8,128)(2,1)} %w_value.1, ...), custom_call_target="tpu_custom_call" | custom-call | flops 20000000000 | bytes 20000000 | tf_op jit(solution)/shard_map/pallas_call | solution.py:700
  171.6 3.1 %copy.12 = bf16[4,256,1024]{2,1,0:T(8,128)(2,1)} copy(bf16[4,256,1024]{2,1,0:T(8,128)(2,1)} %shard_map.100) | data formatting | bytes 4194304

commit v6 on v4

--- a/solution.py
+++ b/solution.py
@@ -465,6 +465,9 @@
     def wait_send(n, j):
         up_copy(n, j).wait_send()
 
+    near = inner & owns_first
+    distant = inner & jnp.logical_not(owns_first)
+
     @pl.loop(0, rounds + 4)
     def _(u):
         @pl.when(u < rounds)
@@ -498,17 +501,26 @@
             def _():
                 end_copy(j).start()
 
-        @pl.when(u == 4)
-        def _():
-            @pl.when(spreads_first)
-            def _():
-                w_copy(0).wait_recv()
-                spread_start(0)
-
-            @pl.when(inner)
-            def _():
-                end_w_direct(1).wait_recv()
-                spread_start(3)
+        @pl.when((u == 4) & near)
+        def _():
+            end_w_direct(0).wait_recv()
+            spread_start(2)
+            end_w_direct(1).wait_recv()
+            spread_start(3)
+
+        @pl.when((u == 4) & spreads_first)
+        def _():
+            w_copy(0).wait_recv()
+            spread_start(0)
+
+        @pl.when((u == 7) & distant)
+        def _():
+            end_w_direct(1).wait_recv()
+            spread_start(3)
+
+        @pl.when((u == 9) & distant)
+        def _():
+            spread_far(3)
 
         @pl.when(u == 8)
         def _():
@@ -525,15 +537,17 @@
             loads[4].wait()
             loads[5].wait()
 
-            @pl.when(spreads_first)
-            def _():
-                spread_end(0)
-
-            @pl.when(inner)
-            def _():
-                spread_far(3)
+            @pl.when(distant)
+            def _():
                 end_w_direct(0).wait_recv()
                 spread_start(2)
+
+            @pl.when(spreads_first)
+            def _():
+                spread_end(0)
+
+            @pl.when(inner)
+            def _():
                 spread_end(2)
 
         @pl.when((u >= 5) & (u % 2 == 1) & inner)
@@ -542,11 +556,12 @@
             end_copy(j).wait_recv()
             joint_step(first, 0, j)
 
-            @pl.when(j == 0)
-            def _():
+            @pl.when((j == 0) & near)
+            def _():
+                spread_far(3)
                 spread_end(3)
 
-            @pl.when(third != mp)
+            @pl.when(near)
             def _():
                 joint_step(third, 1, j)
 
@@ -557,6 +572,10 @@
     hidden_load.start()
 
     spread_end(1)
+
+    @pl.when(distant)
+    def _():
+        spread_end(3)
 
     @pl.when(is_end)
     def _():

time: 166 us -> 176 us (1.060)
  Pallas kernels: 162 us -> 173 us
    pallas_call x1, Pallas kernels: 162 us -> 173 us  [fused_shards(): pl.pallas_call(fused_kernel, out_shape=jax.ShapeDtypeStruct(queries.shape...]
where the time goes in v6:
time: 176 us
  Pallas kernels  173 us (98%)
  local copies, waits for them, and re-layouts  3.08 us (2%)
    pallas_call x1, Pallas kernels, fused_shards(): pl.pallas_call(fused_kernel, out_shape=jax.ShapeDtypeStruct(queries.shape...  173 us

profile of v6, /device:TPU:12, one launch (start us, length us, event | category | flops | bytes accessed | tf_op | source)
XLA Modules:
  0.0 176.1 jit_solution(9740310343478329388)
XLA Ops:
  0.0 173.0 %shard_map.100 = bf16[4,256,1024]{2,1,0:T(8,128)(2,1)} custom-call(s32[16]{0:T(128)} %image_caption.1, s32[16]{0:T(128)} %caption_lengths.1, f32[1,1024]{1,0:T(1,128)} %bitcast.1, f32[4,1024]{1,0:T(4,128)} %gate.1, bf16[8,128,1024]{2,1,0:T(8,128)(2,1)} %captions.1, bf16[1024,1024]{1,0:T(8,128)(2,1)} %w_key.1, bf16[1024,1024]{1,0:T(8,128)(2,1)} %w_value.1, ...), custom_call_target="tpu_custom_call" | custom-call | flops 20000000000 | bytes 20000000 | tf_op jit(solution)/shard_map/pallas_call | solution.py:677
  173.0 3.1 %copy.12 = bf16[4,256,1024]{2,1,0:T(8,128)(2,1)} copy(bf16[4,256,1024]{2,1,0:T(8,128)(2,1)} %shard_map.100) | data formatting | bytes 4194304

commit v7 on v6

--- a/solution.py
+++ b/solution.py
@@ -157,6 +157,22 @@
             device_id_type=MESH,
         )
 
+    def w_piece(i):
+        block = 2 * seq + seq
+        part = part_of(2 * core + i, quarter)
+        return pltpu.make_async_remote_copy(
+            src_ref=w_out.at[part, pl.ds(pl.multiple_of(seq * width, width), width)],
+            dst_ref=out_w.at[block, part],
+            send_sem=w_ssem.at[2 * i],
+            recv_sem=w_rsem.at[2 * i],
+            device_id=device(seq_id),
+            device_id_type=MESH,
+        )
+
+    def w_first_wait():
+        w_piece(0).wait_recv()
+        w_piece(1).wait_recv()
+
     is_end = (mp == 0) | (mp == 3)
     first = jnp.where(mp < 2, 3, 0)
     third = 1 + seq
@@ -173,11 +189,12 @@
             device_id=device({"mp": inward}), device_id_type=MESH,
         )
 
-    def end_w_received():
-        return pltpu.make_async_remote_copy(
-            src_ref=out_w.at[first, half_rows],
-            dst_ref=end_w.at[0, half_rows],
-            send_sem=ew_ssem.at[0], recv_sem=ew_rsem.at[0],
+    def end_w_received(i):
+        part = part_of(2 * core + i, quarter)
+        return pltpu.make_async_remote_copy(
+            src_ref=out_w.at[first, part],
+            dst_ref=end_w.at[0, part],
+            send_sem=ew_ssem.at[2 * i], recv_sem=ew_rsem.at[2 * i],
             device_id=device({"mp": inward}), device_id_type=MESH,
         )
 
@@ -234,7 +251,7 @@
             device_id=device({"mp": inward}), device_id_type=MESH,
         )
 
-    w_copy(0).start()
+    w_piece(0).start()
 
     @pl.when(is_end)
     def _():
@@ -482,10 +499,15 @@
         def _():
             stage_rows(u - 2)
 
-        @pl.when((u == 3) & is_end & jnp.logical_not(owns_first))
-        def _():
-            w_copy(0).wait_recv()
-            end_w_received().start()
+        @pl.when(u == 1)
+        def _():
+            w_piece(1).start()
+
+        for i in range(2):
+            @pl.when((u == 2 + i) & is_end & jnp.logical_not(owns_first))
+            def _():
+                w_piece(i).wait_recv()
+                end_w_received(i).start()
 
         @pl.when((u >= 4) & (u % 2 == 0))
         def _():
@@ -510,17 +532,13 @@
 
         @pl.when((u == 4) & spreads_first)
         def _():
-            w_copy(0).wait_recv()
+            w_first_wait()
             spread_start(0)
 
-        @pl.when((u == 7) & distant)
+        @pl.when((u == 4) & distant)
         def _():
             end_w_direct(1).wait_recv()
             spread_start(3)
-
-        @pl.when((u == 9) & distant)
-        def _():
-            spread_far(3)
 
         @pl.when(u == 8)
         def _():
@@ -539,7 +557,8 @@
 
             @pl.when(distant)
             def _():
-                end_w_direct(0).wait_recv()
+                end_w_received(0).wait_recv()
+                end_w_received(1).wait_recv()
                 spread_start(2)
 
             @pl.when(spreads_first)
@@ -556,7 +575,7 @@
             end_copy(j).wait_recv()
             joint_step(first, 0, j)
 
-            @pl.when((j == 0) & near)
+            @pl.when(j == 0)
             def _():
                 spread_far(3)
                 spread_end(3)
@@ -572,10 +591,6 @@
     hidden_load.start()
 
     spread_end(1)
-
-    @pl.when(distant)
-    def _():
-        spread_end(3)
 
     @pl.when(is_end)
     def _():
@@ -609,8 +624,10 @@
     def _(j):
         final_step(j)
 
-    for step in range(2):
-        w_copy(step).wait_send()
+    for i in range(2):
+        w_piece(i).wait_send()
+
+    w_copy(1).wait_send()
 
     spread_sent(1)
 
@@ -626,8 +643,16 @@
 
     @pl.when(is_end)
     def _():
-        for step in range(2):
-            end_w_direct(step).wait_send()
+        end_w_direct(1).wait_send()
+
+        @pl.when(owns_first)
+        def _():
+            end_w_direct(0).wait_send()
+
+        @pl.when(jnp.logical_not(owns_first))
+        def _():
+            end_w_received(0).wait_send()
+            end_w_received(1).wait_send()
 
         for j in range(images):
             end_copy(j).wait_send()
@@ -700,10 +725,10 @@
             dma((rounds,)), dma((rounds,)),
             dma((rounds,)), dma((rounds,)),
             dma((rounds,)), dma((rounds,)),
-            dma((2,)), dma((2,)),
+            dma((3,)), dma((3,)),
             dma((4, images)), dma((4, images)), dma((images,)),
             dma((images,)), dma((images,)),
-            dma((2,)), dma((2,)),
+            dma((3,)), dma((3,)),
             dma((4,)), dma((4,)), dma((4, 2)), dma((4, 2)),
         ],
         compiler_params=pltpu.CompilerParams(

time: 176 us -> 163 us (0.926)
  Pallas kernels: 173 us -> 159 us
    pallas_call x1, Pallas kernels: 173 us -> 159 us  [fused_shards(): pl.pallas_call(fused_kernel, out_shape=jax.ShapeDtypeStruct(queries.shape...]
where the time goes in v7:
time: 163 us; the launch traced here: 162 us
  Pallas kernels  159 us (98%)
  local copies, waits for them, and re-layouts  3.08 us (2%)
    pallas_call x1, Pallas kernels, fused_shards(): pl.pallas_call(fused_kernel, out_shape=jax.ShapeDtypeStruct(queries.shape...  159 us

profile of v7, /device:TPU:12, one launch (start us, length us, event | category | flops | bytes accessed | tf_op | source)
XLA Modules:
  0.0 161.7 jit_solution(1806365385440005416)
XLA Ops:
  0.0 158.6 %shard_map.100 = bf16[4,256,1024]{2,1,0:T(8,128)(2,1)} custom-call(s32[16]{0:T(128)} %image_caption.1, s32[16]{0:T(128)} %caption_lengths.1, f32[1,1024]{1,0:T(1,128)} %bitcast.1, f32[4,1024]{1,0:T(4,128)} %gate.1, bf16[8,128,1024]{2,1,0:T(8,128)(2,1)} %captions.1, bf16[1024,1024]{1,0:T(8,128)(2,1)} %w_key.1, bf16[1024,1024]{1,0:T(8,128)(2,1)} %w_value.1, ...), custom_call_target="tpu_custom_call" | custom-call | flops 20000000000 | bytes 20000000 | tf_op jit(solution)/shard_map/pallas_call | solution.py:702
  158.6 3.1 %copy.12 = bf16[4,256,1024]{2,1,0:T(8,128)(2,1)} copy(bf16[4,256,1024]{2,1,0:T(8,128)(2,1)} %shard_map.100) | data formatting | bytes 4194304
